TPU v7x, 128 devices: a whole 4x4x4 slice. The times are simulated.
128 devices in a mesh: seq: 2 (over core), fsdp: 64 (over z, y, x).
Axes of the slice: x: 4, y: 4, z: 4, core: 2. Of those that a mesh axis runs over, the one named last changes fastest.
Arguments:
- latent_q: bfloat16 [8192, 1536], P(('seq', 'fsdp')), may hold values from -16 to 16
- latent_kv: bfloat16 [8192, 512], P(('seq', 'fsdp')), may hold values from -16 to 16
- grad_q_heads: bfloat16 [8192, 12288], P('seq', 'fsdp')
- grad_kv_heads: bfloat16 [8192, 16384], P('seq', 'fsdp')
- row_peak: float32 [64, 8192], P('fsdp', 'seq'), may hold values from 1 to 400
- momentum_q: float32 [64, 1536, 192], P('fsdp', 'seq'), may hold values from -6 to 6
- momentum_kv: float32 [64, 512, 256], P('fsdp', 'seq'), may hold values from -6 to 6
- weight_q: float32 [64, 1536, 192], P('fsdp', 'seq'), may hold values from -3 to 3
- weight_kv: float32 [64, 512, 256], P('fsdp', 'seq'), may hold values from -3 to 3
Outputs:
- new_momentum_q: float32 [64, 1536, 192], P('fsdp', 'seq')
- new_momentum_kv: float32 [64, 512, 256], P('fsdp', 'seq')
- update_q: float32 [64, 1536, 192], P('fsdp', 'seq')
- update_kv: float32 [64, 512, 256], P('fsdp', 'seq')
- new_weight_q: float32 [64, 1536, 192], P('fsdp', 'seq')
- new_weight_kv: float32 [64, 512, 256], P('fsdp', 'seq')
All inputs are finite; a program needn't handle non-finite values.
Results may differ from a plain program's by a relative error of at most 0.0003.
Values may be sent and summed in bfloat16 or wider, within the bound.
No kernel may reach another device: no remote copies, remote signals or barrier semaphores. Data moves between devices by JAX's collectives and lax.ppermute only.
A program may use at most 128 MiB of HBM per device.

v0:
```python
import functools
import math

import jax
import jax.numpy as jnp
from jax import lax
from jax.experimental import pallas as pl
from jax.experimental.pallas import tpu as pltpu
from jax.sharding import PartitionSpec as P

QN = 128
KN = 128
NS_STEPS = 5

coef_a = 3.4445
coef_b = -4.775
coef_c = 2.0315
momentum_rate = 0.95
learn_rate = 0.1
clip_target = 100.0
norm_eps = 1e-07

F32 = jnp.float32
BF16 = jnp.bfloat16


def dot(left, right, left_dim=1, right_dim=0):
    return lax.dot_general(
        left, right, (((left_dim,), (right_dim,)), ((), ())), preferred_element_type=F32
    )


def halves(value):
    high = value.astype(BF16)
    return high, (value - high.astype(F32)).astype(BF16)


def product(left, right):
    (lh, ll), (rh, rl) = left, right
    return dot(lh, rh) + (dot(lh, rl) + dot(ll, rh))


def gram_of(parts):
    high, low = parts
    cross = dot(high, low, 1, 1)
    return dot(high, high, 1, 1) + (cross + cross.T)


def sweep(iterate):
    parts = halves(iterate)
    gram = gram_of(parts)
    gram_parts = halves(gram)
    poly = coef_b * gram + coef_c * product(gram_parts, gram_parts)
    return coef_a * iterate + product(halves(poly), parts)


def normalized(matrix):
    norm = jnp.sqrt(jnp.sum(matrix * matrix))
    return matrix / (norm + norm_eps)


def finish_kernel(
    core_ref,
    root_ref,
    factor_ref,
    own_q_ref,
    other_q_ref,
    mom_q_ref,
    weight_q_ref,
    own_kv_ref,
    other_kv_ref,
    mom_kv_ref,
    weight_kv_ref,
    out_mom_q_ref,
    out_mom_kv_ref,
    out_upd_q_ref,
    out_upd_kv_ref,
    out_weight_q_ref,
    out_weight_kv_ref,
    full_q_ref,
    full_kv_ref,
):
    core = core_ref[0]
    root = root_ref[0]
    factor = factor_ref[0]
    shard_q = out_mom_q_ref.shape[1]
    shard_kv = out_mom_kv_ref.shape[0]
    cols_q = pl.ds(pl.multiple_of(core * shard_q, 128), shard_q)
    cols_kv = pl.ds(pl.multiple_of(core * shard_kv, 128), shard_kv)
    mom_q = momentum_rate * mom_q_ref[...] + (own_q_ref[...] + other_q_ref[...])
    mom_kv = momentum_rate * mom_kv_ref[...] + (own_kv_ref[...] + other_kv_ref[...])
    full_q_ref[...] = mom_q
    full_kv_ref[...] = mom_kv
    out_mom_q_ref[...] = full_q_ref[:, cols_q]
    out_mom_kv_ref[...] = full_kv_ref[:, cols_kv].T
    x_q = normalized(mom_q)
    x_kv = normalized(mom_kv)
    for _ in range(NS_STEPS):
        x_q = sweep(x_q)
        x_kv = sweep(x_kv)
    full_q_ref[...] = x_q
    full_kv_ref[...] = x_kv
    upd_q = (0.2 * math.sqrt(x_q.shape[1])) * full_q_ref[:, cols_q]
    out_upd_q_ref[...] = upd_q
    rows = lax.broadcasted_iota(jnp.int32, upd_q.shape, 0)
    scale_q = jnp.where(rows < QN, root, factor)
    out_weight_q_ref[...] = (weight_q_ref[...] - learn_rate * upd_q) * scale_q
    upd_kv = ((0.2 * math.sqrt(x_kv.shape[1])) * full_kv_ref[:, cols_kv]).T
    out_upd_kv_ref[...] = upd_kv
    lanes = lax.broadcasted_iota(jnp.int32, upd_kv.shape, 1)
    scale_kv = jnp.where(lanes < KN, root, 1.0)
    out_weight_kv_ref[...] = (weight_kv_ref[...] - learn_rate * upd_kv) * scale_kv


def finish(core, root, factor, *arrays):
    own_q, _, _, weight_q, own_kv, _, _, weight_kv = arrays
    smem = pl.BlockSpec(memory_space=pltpu.SMEM)
    vmem = pl.BlockSpec(memory_space=pltpu.VMEM)
    shape_q = jax.ShapeDtypeStruct(weight_q.shape, F32)
    shape_kv = jax.ShapeDtypeStruct(weight_kv.shape, F32)
    return pl.pallas_call(
        finish_kernel,
        out_shape=(shape_q, shape_kv) * 3,
        in_specs=[smem] * 3 + [vmem] * 8,
        out_specs=(vmem,) * 6,
        scratch_shapes=[pltpu.VMEM(own_q.shape, F32), pltpu.VMEM(own_kv.shape, F32)],
        compiler_params=pltpu.CompilerParams(vmem_limit_bytes=48 * 1024 * 1024),
        cost_estimate=pl.CostEstimate(
            flops=20_000_000_000, bytes_accessed=12_000_000, transcendentals=0
        ),
    )(core, root, factor, *arrays)


def swap(value):
    return lax.ppermute(value, "seq", [(0, 1), (1, 0)])


def joined(core, own, axis):
    other = swap(own)
    return jnp.where(
        core == 0,
        jnp.concatenate([own, other], axis=axis),
        jnp.concatenate([other, own], axis=axis),
    )


def on_device(
    latent_q,
    latent_kv,
    grad_q_heads,
    grad_kv_heads,
    row_peak,
    momentum_q,
    momentum_kv,
    weight_q,
    weight_kv,
):
    core = lax.axis_index("seq")
    rank_q = latent_q.shape[1]
    latents = lax.all_gather(
        jnp.concatenate([latent_q, latent_kv], axis=1), "fsdp", axis=0, tiled=True
    )
    peak_own = jnp.max(row_peak, axis=1)
    peak = jnp.maximum(peak_own, swap(peak_own))
    factor = jnp.minimum(1.0, clip_target / peak)
    root = jnp.sqrt(factor)
    mom_q = joined(core, momentum_q[0].T, 1)
    mom_kv = joined(core, momentum_kv[0].T, 1)
    own_q = dot(grad_q_heads.T, latents[:, :rank_q])
    own_kv = dot(grad_kv_heads.T, latents[:, rank_q:])
    outs = finish(
        core.reshape(1),
        root,
        factor,
        own_q,
        swap(own_q),
        mom_q,
        weight_q[0].T,
        own_kv,
        swap(own_kv),
        mom_kv,
        weight_kv[0],
    )
    new_mom_q, new_mom_kv, upd_q, upd_kv, new_weight_q, new_weight_kv = outs
    return (
        new_mom_q.T[None],
        new_mom_kv[None],
        upd_q.T[None],
        upd_kv[None],
        new_weight_q.T[None],
        new_weight_kv[None],
    )


def solution(mesh):
    rows = P("fsdp", "seq", None)
    placed = (
        P(("seq", "fsdp"), None),
        P(("seq", "fsdp"), None),
        P("seq", "fsdp"),
        P("seq", "fsdp"),
        P("fsdp", "seq"),
        rows,
        rows,
        rows,
        rows,
    )
    return jax.shard_map(
        on_device, mesh=mesh, in_specs=placed, out_specs=(rows,) * 6, check_vma=False
    )
```

profile of v0, /device:TPU:1, one launch (start us, length us, event | category | flops | bytes accessed | tf_op | source)
XLA Modules:
  0.0 160.2 jit_solution(7545951187419000684)
XLA Ops:
  7.2 0.0 copy-start
  7.2 0.0 all-gather.2.cloned.1.call-start
  7.2 1.8 %pad_maximum_fusion = bf16[64,2048]{1,0:T(8,128)(2,1)} fusion(bf16[64,512]{1,0:T(8,128)(2,1)} %param.10, bf16[64,1536]{1,0:T(8,128)(2,1)} %param.9), kind=kLoop, calls=%fused_computation.8 | loop fusion | flops 524288 | bytes 524288 | tf_op jit(solution)/shard_map/concatenate | solution.py:161
  9.0 0.0 all-gather.2.cloned.1.call-update
  9.1 110.0 %all-gather.2.cloned.1.call-done = bf16[4096,2048]{1,0:T(8,128)(2,1)} async-done(((bf16[64,2048]{1,0:T(8,128)(2,1)}), bf16[4096,2048]{1,0:T(8,128)(2,1)}) %all-gather.2.cloned.1.call-update) | async-done | bytes 16777232 | tf_op jit(solution)/shard_map/all_gather | solution.py:160
  119.1 6.5 %fusion.4.own_q_ref = f32[192,1536]{1,0:T(8,128)S(1)} fusion(bf16[4096,192]{0,1:T(8,128)(2,1)} %param.11, bf16[4096,2048]{1,0:T(8,128)(2,1)} %all-gather.2.cloned.1.call-done), kind=kOutput, calls=%fused_computation.4 | convolution fusion | flops 2415919104 | bytes 15335424 | tf_op jit(solution)/shard_map/dot_general | solution.py:28
  125.6 0.8 collective-permute-start.1
  126.3 1.1 copy.16
  127.4 0.1 collective-permute-start.4
  127.5 0.0 copy-start.3
  127.5 0.5 collective-permute-start.2
  128.0 0.0 copy-done
  128.0 4.3 %fusion.7.own_kv_ref = f32[256,512]{1,0:T(8,128)} fusion(bf16[4096,256]{1,0:T(8,128)(2,1)S(1)} %copy-done, bf16[4096,2048]{1,0:T(8,128)(2,1)} %all-gather.2.cloned.1.call-done), kind=kOutput, calls=%fused_computation.5 | convolution fusion | flops 1073741824 | bytes 6815744 | tf_op jit(solution)/shard_map/dot_general | solution.py:28
  132.3 0.1 collective-permute-start.3
  132.4 0.0 copy-done.3
  132.4 0.6 reduce_max.11
  133.1 0.4 collective-permute-start
  133.5 1.1 collective-permute-done
  135.9 0.0 copy-start.1
  135.9 0.0 copy-start.2
  136.0 0.0 collective-permute-done.4
  136.0 1.2 maximum_select_fusion.1.mom_kv_ref
  137.1 0.0 collective-permute-done.2
  137.1 1.8 %maximum_select_fusion.mom_q_ref = f32[192,1536]{1,0:T(8,128)S(1)} fusion(f32[192,768]{1,0:T(8,128)} %collective-permute-done.2, f32[192,768]{1,0:T(8,128)} %bitcast.35, pred[]{:T(512)S(6)} %eq.4), kind=kLoop, calls=%fused_computation.6 | loop fusion | flops 884736 | bytes 2359297 | tf_op jit(solution)/shard_map/jit(_where)/select_n | solution.py:140
  139.0 0.0 collective-permute-done.3.other_kv_ref
  139.0 0.0 collective-permute-done.1.other_q_ref
  139.0 0.0 copy-done.1
  139.0 0.0 copy-done.2
  139.0 14.3 %shard_map.136 = (f32[192,768]{1,0:T(8,128)}, f32[256,256]{1,0:T(8,128)}, f32[192,768]{1,0:T(8,128)}, f32[256,256]{1,0:T(8,128)}, f32[192,768]{1,0:T(8,128)}, /*index=5*/f32[256,256]{1,0:T(8,128)}) custom-call(s32[1]{0:T(128)} %bitcast.core_ref, f32[1]{0:T(128)S(6)} %sqrt.3.root_ref, f32[1]{0:T(128)S(6)} %min.3.factor_ref, f32[192,1536]{1,0:T(8,128)S(1)} %fusion.4.own_q_ref, ...), custom_call_target="tpu_custom_call" | custom-call | flops 20000000000 | bytes 12000000 | tf_op jit(solution)/shard_map/pallas_call | solution.py:121
Async XLA Ops:
  7.2 120.9 %copy-start = (bf16[4096,256]{1,0:T(8,128)(2,1)S(1)}, bf16[4096,256]{1,0:T(8,128)(2,1)}, u32[]{:S(2)}) copy-start(bf16[4096,256]{1,0:T(8,128)(2,1)} %param.12) | copy-start | bytes 6291460
  7.2 111.9 %all-gather.2.cloned.1.call-start = ((), (), s32[]{:S(2)}) async-start(), calls=%async_computation | async-start | bytes 17039360 | tf_op jit(solution)/shard_map/all_gather | solution.py:160
  125.6 13.4 %collective-permute-start.1 = (f32[192,1536]{1,0:T(8,128)S(1)}, f32[192,1536]{1,0:T(8,128)}, u32[]{:S(2)}, u32[]{:S(2)}) collective-permute-start(f32[192,1536]{1,0:T(8,128)S(1)} %fusion.4.own_q_ref), channel_id=1, source_target_pairs={{0,64},{64,0},{1,65},{65,1},{2,66},{66,2},{3,67},{67,3},{4,68},{68... | collective-permute-start | bytes 3538952 | tf_op jit(solution)/shard_map/ppermute | solution.py:135
  127.4 8.5 %collective-permute-start.4 = (f32[256,256]{1,0:T(8,128)S(1)}, f32[256,256]{1,0:T(8,128)}, u32[]{:S(2)}, u32[]{:S(2)}) collective-permute-start(f32[256,256]{1,0:T(8,128)S(1)} %bitcast.32), channel_id=1, source_target_pairs={{0,64},{64,0},{1,65},{65,1},{2,66},{66,2},{3,67},{67,3},{4,68},{68... | collective-permute-start | bytes 786440 | tf_op jit(solution)/shard_map/ppermute | solution.py:135
  127.5 4.9 %copy-start.3 = (f32[1,4096]{1,0:T(1,128)S(1)}, f32[1,4096]{1,0:T(1,128)}, u32[]{:S(2)}) copy-start(f32[1,4096]{1,0:T(1,128)} %param.13) | copy-start | bytes 49156
  127.5 9.6 %collective-permute-start.2 = (f32[192,768]{1,0:T(8,128)}, f32[192,768]{1,0:T(8,128)}, u32[]{:S(2)}, u32[]{:S(2)}) collective-permute-start(f32[192,768]{1,0:T(8,128)} %bitcast.34), channel_id=1, source_target_pairs={{0,64},{64,0},{1,65},{65,1},{2,66},{66,2},{3,67},{67,3},{4,68},{68... | collective-permute-start | bytes 1769480 | tf_op jit(solution)/shard_map/ppermute | solution.py:135
  132.3 6.7 %collective-permute-start.3 = (f32[256,512]{1,0:T(8,128)}, f32[256,512]{1,0:T(8,128)}, u32[]{:S(2)}, u32[]{:S(2)}) collective-permute-start(f32[256,512]{1,0:T(8,128)} %fusion.7.own_kv_ref), channel_id=1, source_target_pairs={{0,64},{64,0},{1,65},{65,1},{2,66},{66,2},{3,67},{67,3},{4,68},{68... | collective-permute-start | bytes 1572872 | tf_op jit(solution)/shard_map/ppermute | solution.py:135
  133.1 1.5 collective-permute-start
  135.9 3.1 %copy-start.1 = (f32[1,768,192]{1,2,0:T(8,128)S(1)}, f32[1,768,192]{1,2,0:T(8,128)}, u32[]{:S(2)}) copy-start(f32[1,768,192]{1,2,0:T(8,128)} %param.16) | copy-start | bytes 1769476
  135.9 3.1 %copy-start.2 = (f32[1,256,256]{2,1,0:T(8,128)S(1)}, f32[1,256,256]{2,1,0:T(8,128)}, u32[]{:S(2)}) copy-start(f32[1,256,256]{2,1,0:T(8,128)} %param.17) | copy-start | bytes 786436
Sparse Core Ops, SparseCore 0:
  11.5 107.5 all-gather.1
where the time goes:
time: 160 us
  waiting for transfers between devices  111 us (69%)
  between operations  15.5 us (10%)
  Pallas kernels  14.3 us (9%)
  matrix products  10.8 us (7%)
  other arithmetic  5.45 us (3%)
  starting transfers between devices  1.89 us (1%)
    all_gather x1, waiting for transfers between devices, on_device(): lax.all_gather(jnp.concatenate([latent_q, latent_kv], axis=1), 'fsdp', ax...  110 us
    pallas_call x1, Pallas kernels, finish(): pl.pallas_call(finish_kernel, out_shape=(shape_q, shape_kv) * 3, in_specs...  14.3 us
    dot_general x2, matrix products, dot(): lax.dot_general(left, right, (((left_dim,), (right_dim,)), ((), ())), pre...  10.8 us
  transfers between devices with their start and end apart: 6, of which 2 were waited for; matrix products, arithmetic and copies ran while one was open for 6% of the time, Pallas kernels for 0%

commit v1 on v0

v1 whole, which is shorter than its diff:
```python
import functools
import math

import jax
import jax.numpy as jnp
import numpy as np
from jax import lax
from jax.experimental import pallas as pl
from jax.experimental.pallas import tpu as pltpu
from jax.sharding import PartitionSpec as P

QN = 128
KN = 128
NS_STEPS = 5

coef_a = 3.4445
coef_b = -4.775
coef_c = 2.0315
momentum_rate = 0.95
learn_rate = 0.1
clip_target = 100.0
norm_eps = 1e-07

F32 = jnp.float32
BF16 = jnp.bfloat16

CHIPS = 64
RING = 4
PARTS = 3
STRIDES = {"z": 16, "y": 4, "x": 1}
AXES = (("xyz", "yzx", "zxy"), ("yzx", "zxy", "xyz"))
HOPS = ((1, 3), (3, 1))
SMEM = pl.BlockSpec(memory_space=pltpu.SMEM)
VMEM = pl.BlockSpec(memory_space=pltpu.VMEM)
MIB = 1024 * 1024


def dot(left, right, left_dim=1, right_dim=0):
    return lax.dot_general(
        left, right, (((left_dim,), (right_dim,)), ((), ())), preferred_element_type=F32
    )


def halves(value):
    high = value.astype(BF16)
    return high, (value - high.astype(F32)).astype(BF16)


def product(left, right):
    (lh, ll), (rh, rl) = left, right
    return dot(lh, rh) + (dot(lh, rl) + dot(ll, rh))


def gram_of(parts):
    high, low = parts
    cross = dot(high, low, 1, 1)
    return dot(high, high, 1, 1) + (cross + cross.T)


def sweep(iterate):
    parts = halves(iterate)
    gram = gram_of(parts)
    gram_parts = halves(gram)
    poly = coef_b * gram + coef_c * product(gram_parts, gram_parts)
    return coef_a * iterate + product(halves(poly), parts)


def normalized(matrix):
    norm = jnp.sqrt(jnp.sum(matrix * matrix, keepdims=True))
    return matrix / (norm + norm_eps)


class Layout:
    def __init__(self, width_q, width_kv, rank_q, rank_kv):
        unit_q, unit_kv = rank_q // PARTS, rank_kv // 4
        starts = (0, 2, 3, 4)
        self.width_q, self.width_kv = width_q, width_kv
        self.rank_q, self.rank_kv = rank_q, rank_kv
        self.q = [(p * unit_q, unit_q) for p in range(PARTS)]
        self.kv = [
            (starts[p] * unit_kv, (starts[p + 1] - starts[p]) * unit_kv) for p in range(PARTS)
        ]
        self.pack_width = unit_q

    def bands(self, part):
        wide = self.kv[part][1]
        count = self.pack_width // wide
        tall = self.width_kv // count
        return [(i * tall, tall, i * wide, wide) for i in range(count)]

    def pack_shape(self, part):
        return (self.width_q + self.bands(part)[0][1], self.pack_width)


def swap(value):
    return lax.ppermute(value, "seq", [(0, 1), (1, 0)])


def after(values, earlier):
    return lax.optimization_barrier((values, earlier))[0]


def exchange(value, part, phase, step):
    pairs = []
    for core in range(2):
        stride = STRIDES[AXES[core][part][phase]]
        for chip in range(CHIPS):
            at = chip // stride % RING
            other = chip + ((at ^ HOPS[core][step]) - at) * stride
            pairs.append((core * CHIPS + chip, core * CHIPS + other))
    return lax.ppermute(value, ("seq", "fsdp"), pairs)


def block_orders():
    table = np.zeros((2 * CHIPS, PARTS * CHIPS), np.int32)
    for core in range(2):
        first, second = HOPS[core]
        order = (0, first, second, first ^ second)
        for chip in range(CHIPS):
            for part in range(PARTS):
                for slot in range(CHIPS):
                    chosen = chip
                    for phase in range(3):
                        stride = STRIDES[AXES[core][part][phase]]
                        at = chip // stride % RING
                        turn = order[slot // RING**phase % RING]
                        chosen += ((at ^ turn) - at) * stride
                    table[core * CHIPS + chip, part * CHIPS + slot] = chosen
    return table


def arrange_kernel(order_ref, grad_q_ref, grad_kv_ref, *outs):
    rows = grad_kv_ref.shape[0] // CHIPS
    width_q = grad_q_ref.shape[0]
    pair = 2 * rows
    left = lax.broadcasted_iota(jnp.int32, (width_q, pair), 1) < rows

    def query_pair(first, second):
        turned = []
        for block, half in ((first, 0), (second, 1)):
            tile = grad_q_ref[:, pl.ds(pl.multiple_of(block // 2 * pair, pair), pair)]
            tile = tile.astype(F32)
            turned.append(jnp.where(block % 2 == half, tile, pltpu.roll(tile, rows, 1)))
        return jnp.where(left, turned[0], turned[1]).astype(BF16)

    for part in range(PARTS):
        for slot in range(RING):
            out = outs[part + PARTS * (slot % 2)]

            @pl.loop(0, RING)
            def _(chunk):
                base = part * CHIPS + slot * 16 + chunk * RING
                start = (slot // 2) * 16 * rows + chunk * (RING * rows)
                at = [order_ref[base + k] for k in range(RING)]
                for k in range(0, RING, 2):
                    lanes = pl.ds(pl.multiple_of(start + k * rows, pair), pair)
                    out[:width_q, lanes] = query_pair(at[k], at[k + 1])
                spans = [pl.ds(pl.multiple_of(block * rows, rows), rows) for block in at]
                whole = jnp.concatenate([grad_kv_ref[span, :] for span in spans], axis=0)
                lanes = pl.ds(pl.multiple_of(start, RING * rows), RING * rows)
                out[width_q:, lanes] = whole.T


def arrange(order, grad_q, grad_kv):
    shape = (grad_q.shape[0] + grad_kv.shape[1], grad_kv.shape[0] // 2)
    outs = pl.pallas_call(
        arrange_kernel,
        out_shape=(jax.ShapeDtypeStruct(shape, BF16),) * (2 * PARTS),
        in_specs=[SMEM, VMEM, VMEM],
        out_specs=(VMEM,) * (2 * PARTS),
        compiler_params=pltpu.CompilerParams(vmem_limit_bytes=24 * MIB),
        cost_estimate=pl.CostEstimate(
            flops=0, bytes_accessed=20_000_000, transcendentals=0
        ),
    )(order, grad_q, grad_kv)
    return outs[:PARTS], outs[PARTS:]


def multiply_kernel(layout, half, count_in, *refs):
    pieces, grads = refs[:PARTS], refs[PARTS : 2 * PARTS]
    sums, outs = refs[2 * PARTS : 2 * PARTS + count_in], refs[-PARTS:]
    span = pieces[0].shape[0]
    lanes = pl.ds(half * span, span)
    tall_q = layout.width_q
    for part in range(PARTS):
        wide_q = layout.q[part][1]
        term_q = dot(grads[part][:tall_q, lanes], pieces[part][:, :wide_q])
        term_kv = dot(grads[part][tall_q:, lanes], pieces[part][:, wide_q:])
        spots = [((0, tall_q), (0, wide_q), term_q)]
        for top, tall, at, wide in layout.bands(part):
            spots.append(((tall_q, tall), (at, wide), term_kv[top : top + tall, :]))
        for rows, cols, term in spots:
            where = (pl.ds(*rows), pl.ds(*cols))
            outs[part][where] = term + sums[part][where] if count_in else term


def multiply(layout, half, pieces, grads, sums=()):
    operands = [*pieces, *grads, *sums]
    return pl.pallas_call(
        functools.partial(multiply_kernel, layout, half, len(sums)),
        out_shape=tuple(
            jax.ShapeDtypeStruct(layout.pack_shape(p), F32) for p in range(PARTS)
        ),
        in_specs=[VMEM] * len(operands),
        out_specs=(VMEM,) * PARTS,
        compiler_params=pltpu.CompilerParams(vmem_limit_bytes=32 * MIB),
        cost_estimate=pl.CostEstimate(
            flops=2_000_000_000, bytes_accessed=8_000_000, transcendentals=0
        ),
    )(*operands)


def finish_kernel(layout, core_ref, *refs):
    packs = [refs[i * PARTS : (i + 1) * PARTS] for i in range(4)]
    (
        peak_ref,
        peak_other_ref,
        mom_q_ref,
        mom_q_other_ref,
        mom_kv_ref,
        mom_kv_other_ref,
        weight_q_ref,
        weight_kv_ref,
        out_mom_q_ref,
        out_mom_kv_ref,
        out_upd_q_ref,
        out_upd_kv_ref,
        out_weight_q_ref,
        out_weight_kv_ref,
        full_q_ref,
        full_kv_ref,
    ) = refs[4 * PARTS :]
    core = core_ref[0]
    peak = jnp.maximum(
        jnp.max(peak_ref[...], keepdims=True), jnp.max(peak_other_ref[...], keepdims=True)
    )
    factor = jnp.minimum(1.0, clip_target / peak)
    root = jnp.sqrt(factor)

    def lanes(at, ref):
        return pl.ds(pl.multiple_of(at * ref.shape[1] // 2, 128), ref.shape[1] // 2)

    own_q, other_q = lanes(core, full_q_ref), lanes(1 - core, full_q_ref)
    own_kv, other_kv = lanes(core, full_kv_ref), lanes(1 - core, full_kv_ref)
    full_q_ref[:, own_q] = momentum_rate * mom_q_ref[...]
    full_q_ref[:, other_q] = momentum_rate * mom_q_other_ref[...]
    full_kv_ref[:, own_kv] = momentum_rate * mom_kv_ref[...].T
    full_kv_ref[:, other_kv] = momentum_rate * mom_kv_other_ref[...].T
    tall_q = layout.width_q
    for part in range(PARTS):
        own, own_swapped, got, got_swapped = [pack[part] for pack in packs]

        def total(rows, cols):
            where = (pl.ds(*rows), pl.ds(*cols))
            return (own[where] + own_swapped[where]) + (got[where] + got_swapped[where])

        at_q, wide_q = layout.q[part]
        full_q_ref[:, pl.ds(at_q, wide_q)] += total((0, tall_q), (0, wide_q))
        at_kv, wide_kv = layout.kv[part]
        for top, tall, at, wide in layout.bands(part):
            full_kv_ref[pl.ds(top, tall), pl.ds(at_kv, wide_kv)] += total(
                (tall_q, tall), (at, wide)
            )
    out_mom_q_ref[...] = full_q_ref[:, own_q]
    out_mom_kv_ref[...] = full_kv_ref[:, own_kv].T
    x_q = normalized(full_q_ref[...])
    x_kv = normalized(full_kv_ref[...])
    for _ in range(NS_STEPS):
        x_q = sweep(x_q)
        x_kv = sweep(x_kv)
    full_q_ref[...] = x_q
    full_kv_ref[...] = x_kv
    upd_q = (0.2 * math.sqrt(layout.rank_q)) * full_q_ref[:, own_q]
    out_upd_q_ref[...] = upd_q
    rows = lax.broadcasted_iota(jnp.int32, upd_q.shape, 0)
    scale_q = jnp.where(rows < QN, root, factor)
    out_weight_q_ref[...] = (weight_q_ref[...] - learn_rate * upd_q) * scale_q
    upd_kv = ((0.2 * math.sqrt(layout.rank_kv)) * full_kv_ref[:, own_kv]).T
    out_upd_kv_ref[...] = upd_kv
    columns = lax.broadcasted_iota(jnp.int32, upd_kv.shape, 1)
    scale_kv = jnp.where(columns < KN, root, 1.0)
    out_weight_kv_ref[...] = (weight_kv_ref[...] - learn_rate * upd_kv) * scale_kv


def finish(layout, core, packs, *arrays):
    weight_q, weight_kv = arrays[-2:]
    shape_q = jax.ShapeDtypeStruct(weight_q.shape, F32)
    shape_kv = jax.ShapeDtypeStruct(weight_kv.shape, F32)
    operands = [piece for pack in packs for piece in pack] + list(arrays)
    return pl.pallas_call(
        functools.partial(finish_kernel, layout),
        out_shape=(shape_q, shape_kv) * 3,
        in_specs=[SMEM] + [VMEM] * len(operands),
        out_specs=(VMEM,) * 6,
        scratch_shapes=[
            pltpu.VMEM((layout.width_q, layout.rank_q), F32),
            pltpu.VMEM((layout.width_kv, layout.rank_kv), F32),
        ],
        compiler_params=pltpu.CompilerParams(vmem_limit_bytes=40 * MIB),
        cost_estimate=pl.CostEstimate(
            flops=20_000_000_000, bytes_accessed=12_000_000, transcendentals=0
        ),
    )(core, *operands)


def on_device(
    latent_q,
    latent_kv,
    grad_q_heads,
    grad_kv_heads,
    row_peak,
    momentum_q,
    momentum_kv,
    weight_q,
    weight_kv,
):
    core = lax.axis_index("seq")
    device = core * CHIPS + lax.axis_index("fsdp")
    layout = Layout(
        momentum_q.shape[2], momentum_kv.shape[2], latent_q.shape[1], latent_kv.shape[1]
    )
    held = [
        jnp.concatenate(
            [latent_q[:, aq : aq + wq], latent_kv[:, ak : ak + wk]], axis=1
        )
        for (aq, wq), (ak, wk) in zip(layout.q, layout.kv)
    ]
    order = lax.dynamic_index_in_dim(jnp.asarray(block_orders()), device, keepdims=False)
    keep, send = arrange(order, grad_q_heads.T, grad_kv_heads)
    for phase in range(2):
        for step in range(2):
            if phase + step == 1:
                held = after(held, send[0])
            got = [exchange(held[p], p, phase, step) for p in range(PARTS)]
            got = lax.optimization_barrier(got)
            held = [jnp.concatenate([held[p], got[p]], axis=0) for p in range(PARTS)]
    partner = [exchange(send[p], p, 2, 0) for p in range(PARTS)]
    third = [exchange(held[p], p, 2, 1) for p in range(PARTS)]
    lent = multiply(layout, 0, held, partner)
    own = multiply(layout, 0, held, keep)
    lent = multiply(layout, 1, third, partner, lent)
    got = [exchange(lent[p], p, 2, 0) for p in range(PARTS)]
    own = multiply(layout, 1, third, keep, own)
    mom_q, mom_kv = momentum_q[0].T, momentum_kv[0]
    row_peak, mom_q, mom_kv = after((row_peak, mom_q, mom_kv), held[0])
    packs = (own, [swap(o) for o in own], got, [swap(g) for g in got])
    outs = finish(
        layout,
        core.reshape(1),
        packs,
        row_peak,
        swap(row_peak),
        mom_q,
        swap(mom_q),
        mom_kv,
        swap(mom_kv),
        weight_q[0].T,
        weight_kv[0],
    )
    new_mom_q, new_mom_kv, upd_q, upd_kv, new_weight_q, new_weight_kv = outs
    return (
        new_mom_q.T[None],
        new_mom_kv[None],
        upd_q.T[None],
        upd_kv[None],
        new_weight_q.T[None],
        new_weight_kv[None],
    )


def solution(mesh):
    rows = P("fsdp", "seq", None)
    placed = (
        P(("seq", "fsdp"), None),
        P(("seq", "fsdp"), None),
        P("seq", "fsdp"),
        P("seq", "fsdp"),
        P("fsdp", "seq"),
        rows,
        rows,
        rows,
        rows,
    )
    return jax.shard_map(
        on_device, mesh=mesh, in_specs=placed, out_specs=(rows,) * 6, check_vma=False
    )
```

time: 160 us -> 131 us (0.82)
  waiting for transfers between devices: 111 us -> 46 us
  starting transfers between devices: 1.89 us -> 50.3 us
  between operations: 15.5 us -> 0.94 us
  Pallas kernels: 14.3 us -> 26.4 us
  matrix products: 10.8 us -> 0 us
  local copies, waits for them, and re-layouts: 1.1 us -> 6.59 us
  other arithmetic: 5.45 us -> 0.33 us
    all_gather x1 -> x0, waiting for transfers between devices: 110 us -> none  [on_device(): lax.all_gather(jnp.concatenate([latent_q, latent_kv], axis=1), 'fsdp', ax...]
    ppermute x0 -> x21, waiting for transfers between devices: none -> 43.8 us  [exchange(): return lax.ppermute(value, ('seq', 'fsdp'), pairs)]
    ppermute x0 -> x21, starting transfers between devices: none -> 25.8 us  [exchange(): return lax.ppermute(value, ('seq', 'fsdp'), pairs)]
    ppermute x5 -> x9, starting transfers between devices: 1.85 us -> 24.5 us  [swap(): return lax.ppermute(value, 'seq', [(0, 1), (1, 0)])]
    pallas_call x1 -> x6, Pallas kernels: 14.3 us -> 26.4 us  [the longest x1 13 us: finish(): pl.pallas_call(functools.partial(finish_kernel, layout), out_shape=(shape...]
    dot_general x2 -> x0, matrix products: 10.8 us -> none  [dot(): lax.dot_general(left, right, (((left_dim,), (right_dim,)), ((), ())), pre...]
    select_n x2 -> x0, other arithmetic: 3 us -> none  [joined(): jnp.where(core == 0, jnp.concatenate([own, other], axis=axis), jnp.concat...]
    slice x0 -> x3, local copies, waits for them, and re-layouts: none -> 2.42 us  [the longest x2 1.5 us: on_device(): latent_kv[:, ak:ak + wk]]
  transfers between devices with their start and end apart: 6 -> 30, of which waited for: 2 -> 16; matrix products, arithmetic and copies ran while one was open for 6% -> 2% of each run, Pallas kernels for 0% -> 10%
where the time goes in v1:
time: 131 us
  starting transfers between devices  50.3 us (38%)
  waiting for transfers between devices  46 us (35%)
  Pallas kernels  26.4 us (20%)
  local copies, waits for them, and re-layouts  6.59 us (5%)
    ppermute x21, waiting for transfers between devices, exchange(): return lax.ppermute(value, ('seq', 'fsdp'), pairs)  43.8 us
    ppermute x21, starting transfers between devices, exchange(): return lax.ppermute(value, ('seq', 'fsdp'), pairs)  25.8 us
    ppermute x9, starting transfers between devices, swap(): return lax.ppermute(value, 'seq', [(0, 1), (1, 0)])  24.5 us
    pallas_call x1, Pallas kernels, finish(): pl.pallas_call(functools.partial(finish_kernel, layout), out_shape=(shape...  13 us
    pallas_call x1, Pallas kernels, arrange(): pl.pallas_call(arrange_kernel, out_shape=(jax.ShapeDtypeStruct(shape, BF1...  8.66 us
    pallas_call x4, Pallas kernels, multiply(): pl.pallas_call(functools.partial(multiply_kernel, layout, half, len(sums)...  4.77 us
    unnamed x20, local copies, waits for them, and re-layouts  3.22 us
  transfers between devices with their start and end apart: 30, of which 16 were waited for; matrix products, arithmetic and copies ran while one was open for 2% of the time, Pallas kernels for 10%

profile of v1, /device:TPU:1, one launch (start us, length us, event | category | flops | bytes accessed | tf_op | source)
XLA Modules:
  0.0 130.5 jit_solution(16928725891888702736)
XLA Ops:
  0.6 0.9 fusion
  1.6 0.7 fusion.1
  2.3 4.7 %collective-permute-start.1 = (bf16[64,640]{1,0:T(8,128)(2,1)S(1)}, bf16[64,640]{1,0:T(8,128)(2,1)S(1)}, u32[]{:S(2)}, u32[]{:S(2)}) collective-permute-start(bf16[64,640]{1,0:T(8,128)(2,1)S(1)} %pad_maximum_fusion.10), channel_id=1, source_target_pairs={{0,4},{1,5},{2,6},{3,7},{4,0},{5,1},{6,2},{7,3},{8,12},{9,13},{10,... | collective-permute-start | bytes 245768 | tf_op jit(solution)/shard_map/ppermute | solution.py:111
  7.0 2.6 %collective-permute-start.2 = (bf16[64,640]{1,0:T(8,128)(2,1)S(1)}, bf16[64,640]{1,0:T(8,128)(2,1)S(1)}, u32[]{:S(2)}, u32[]{:S(2)}) collective-permute-start(bf16[64,640]{1,0:T(8,128)(2,1)S(1)} %pad_maximum_fusion.11), channel_id=1, source_target_pairs={{0,16},{1,17},{2,18},{3,19},{4,20},{5,21},{6,22},{7,23},{8,24},{9,... | collective-permute-start | bytes 245768 | tf_op jit(solution)/shard_map/ppermute | solution.py:111
  9.5 0.8 slice.19
  10.3 2.8 %collective-permute-start = (bf16[64,768]{1,0:T(8,128)(2,1)S(1)}, bf16[64,768]{1,0:T(8,128)(2,1)S(1)}, u32[]{:S(2)}, u32[]{:S(2)}) collective-permute-start(bf16[64,768]{1,0:T(8,128)(2,1)S(1)} %pad_maximum_fusion.9), channel_id=1, source_target_pairs={{0,1},{1,0},{2,3},{3,2},{4,5},{5,4},{6,7},{7,6},{8,9},{9,8},{10,11... | collective-permute-start | bytes 294920 | tf_op jit(solution)/shard_map/ppermute | solution.py:111
  13.1 0.7 constant_dynamic-slice_fusion
  13.8 1.6 %copy-done = bf16[4096,256]{1,0:T(8,128)(2,1)S(1)} copy-done((bf16[4096,256]{1,0:T(8,128)(2,1)S(1)}, bf16[4096,256]{1,0:T(8,128)(2,1)}, u32[]{:S(2)}) %copy-start) | copy-done | bytes 2097176
  15.4 1.4 %copy-done.1 = bf16[4096,192]{0,1:T(8,128)(2,1)S(1)} copy-done((bf16[4096,192]{0,1:T(8,128)(2,1)S(1)}, bf16[4096,192]{0,1:T(8,128)(2,1)}, u32[]{:S(2)}) %copy-start.1) | copy-done | bytes 1572888
  16.8 8.7 %shard_map.145 = (bf16[448,2048]{1,0:T(8,128)(2,1)S(1)}, bf16[448,2048]{1,0:T(8,128)(2,1)S(1)}, bf16[448,2048]{1,0:T(8,128)(2,1)S(1)}, bf16[448,2048]{1,0:T(8,12...) custom-call(s32[192]{0:T(256)S(1)} %bitcast.24, bf16[192,4096]{1,0:T(8,128)(2,1)S(1)} %bitcast.23, ...), custom_call_target="tpu_custom_call" | custom-call | bytes 20000000 | tf_op jit(solution)/shard_map/pallas_call | solution.py:166
  25.6 0.1 collective-permute-start.3
  25.7 0.1 collective-permute-start.4
  25.8 0.1 collective-permute-start.5
  25.9 4.4 %collective-permute-done.4 = bf16[128,640]{1,0:T(8,128)(2,1)S(1)} collective-permute-done((bf16[128,640]{1,0:T(8,128)(2,1)S(1)}, bf16[128,640]{1,0:T(8,128)(2,1)S(1)}, u32[]{:S(2)}, u32[]{:S(2)}) %collective-permute-start.4) | collective-permute-done | bytes 163872 | tf_op jit(solution)/shard_map/ppermute | solution.py:111
  30.2 0.1 collective-permute-done.5
  30.3 0.2 collective-permute-done.3
  30.6 0.1 collective-permute-start.6
  30.7 0.3 collective-permute-start.7
  31.0 0.3 collective-permute-start.8
  31.3 2.5 %collective-permute-start.18 = (bf16[448,2048]{1,0:T(8,128)(2,1)S(1)}, bf16[448,2048]{1,0:T(8,128)(2,1)S(1)}, u32[]{:S(2)}, u32[]{:S(2)}) collective-permute-start(bf16[448,2048]{1,0:T(8,128)(2,1)S(1)} %get-tuple-element.54), channel_id=1, source_target_pairs={{0,16},{1,17},{2,18},{3,19},{4,20},{5,21},{6,22},{7,23},{8,24},{9,... | collective-permute-start | bytes 5505032 | tf_op jit(solution)/shard_map/ppermute | solution.py:111
  33.8 4.1 %collective-permute-done.7 = bf16[256,640]{1,0:T(8,128)(2,1)S(1)} collective-permute-done((bf16[256,640]{1,0:T(8,128)(2,1)S(1)}, bf16[256,640]{1,0:T(8,128)(2,1)S(1)}, u32[]{:S(2)}, u32[]{:S(2)}) %collective-permute-start.7) | collective-permute-done | bytes 327712 | tf_op jit(solution)/shard_map/ppermute | solution.py:111
  37.9 0.2 collective-permute-done.8
  38.1 0.4 collective-permute-done.6
  38.5 0.1 pad_maximum_fusion.2
  38.6 1.2 collective-permute-start.11
  39.8 0.1 pad_maximum_fusion
  39.8 0.9 collective-permute-start.9
  40.8 0.1 pad_maximum_fusion.1
  40.8 0.1 collective-permute-start.10
  40.9 0.1 collective-permute-start.19
  41.1 7.2 %collective-permute-done.11 = bf16[512,640]{1,0:T(8,128)(2,1)S(1)} collective-permute-done((bf16[512,640]{1,0:T(8,128)(2,1)S(1)}, bf16[512,640]{1,0:T(8,128)(2,1)S(1)}, u32[]{:S(2)}, u32[]{:S(2)}) %collective-permute-start.11) | collective-permute-done | bytes 655392 | tf_op jit(solution)/shard_map/ppermute | solution.py:111
  48.4 2.2 %collective-permute-start.20 = (bf16[448,2048]{1,0:T(8,128)(2,1)S(1)}, bf16[448,2048]{1,0:T(8,128)(2,1)S(1)}, u32[]{:S(2)}, u32[]{:S(2)}) collective-permute-start(bf16[448,2048]{1,0:T(8,128)(2,1)S(1)} %get-tuple-element.80), channel_id=1, source_target_pairs={{0,4},{1,5},{2,6},{3,7},{4,0},{5,1},{6,2},{7,3},{8,12},{9,13},{10,... | collective-permute-start | bytes 5505032 | tf_op jit(solution)/shard_map/ppermute | solution.py:111
  50.6 0.0 collective-permute-done.10
  50.7 8.9 %collective-permute-done.9 = bf16[512,768]{1,0:T(8,128)(2,1)S(1)} collective-permute-done((bf16[512,768]{1,0:T(8,128)(2,1)S(1)}, bf16[512,768]{1,0:T(8,128)(2,1)S(1)}, u32[]{:S(2)}, u32[]{:S(2)}) %collective-permute-start.9) | collective-permute-done | bytes 786464 | tf_op jit(solution)/shard_map/ppermute | solution.py:111
  59.5 0.1 constant_dynamic-update-slice_fusion.refs_0_
  59.6 0.1 collective-permute-start.12
  59.7 0.0 copy-start.2
  59.8 0.1 constant_dynamic-update-slice_fusion.6.refs_2_
  59.9 0.9 collective-permute-start.14
  60.8 0.1 constant_dynamic-update-slice_fusion.3.refs_1_
  60.9 3.7 %collective-permute-done.18.refs_3_ = bf16[448,2048]{1,0:T(8,128)(2,1)S(1)} collective-permute-done((bf16[448,2048]{1,0:T(8,128)(2,1)S(1)}, bf16[448,2048]{1,0:T(8,128)(2,1)S(1)}, u32[]{:S(2)}, u32[]{:S(2)}) %collective-permute-start.18) | collective-permute-done | bytes 1835040 | tf_op jit(solution)/shard_map/ppermute | solution.py:111
  64.6 1.2 collective-permute-start.13
  65.8 7.5 %collective-permute-done.19.refs_4_ = bf16[448,2048]{1,0:T(8,128)(2,1)S(1)} collective-permute-done((bf16[448,2048]{1,0:T(8,128)(2,1)S(1)}, bf16[448,2048]{1,0:T(8,128)(2,1)S(1)}, u32[]{:S(2)}, u32[]{:S(2)}) %collective-permute-start.19) | collective-permute-done | bytes 1835040 | tf_op jit(solution)/shard_map/ppermute | solution.py:111
  73.3 6.1 %collective-permute-start.28 = (f32[192,768]{1,0:T(8,128)S(1)}, f32[192,768]{1,0:T(8,128)S(1)}, u32[]{:S(2)}, u32[]{:S(2)}) collective-permute-start(f32[192,768]{1,0:T(8,128)S(1)} %bitcast.25), channel_id=1, source_target_pairs={{0,64},{64,0},{1,65},{65,1},{2,66},{66,2},{3,67},{67,3},{4,68},{68... | collective-permute-start | bytes 1769480 | tf_op jit(solution)/shard_map/ppermute | solution.py:96
  79.4 2.8 %collective-permute-done.20.refs_5_ = bf16[448,2048]{1,0:T(8,128)(2,1)S(1)} collective-permute-done((bf16[448,2048]{1,0:T(8,128)(2,1)S(1)}, bf16[448,2048]{1,0:T(8,128)(2,1)S(1)}, u32[]{:S(2)}, u32[]{:S(2)}) %collective-permute-start.20) | collective-permute-done | bytes 1835040 | tf_op jit(solution)/shard_map/ppermute | solution.py:111
  82.1 15.6 %collective-permute-start.29 = (f32[256,256]{1,0:T(8,128)S(1)}, f32[256,256]{1,0:T(8,128)S(1)}, u32[]{:S(2)}, u32[]{:S(2)}) collective-permute-start(f32[256,256]{1,0:T(8,128)S(1)} %bitcast.28), channel_id=1, source_target_pairs={{0,64},{64,0},{1,65},{65,1},{2,66},{66,2},{3,67},{67,3},{4,68},{68... | collective-permute-start | bytes 786440 | tf_op jit(solution)/shard_map/ppermute | solution.py:96
  97.7 1.2 shard_map.148
  99.0 0.1 collective-permute-start.27
  99.1 1.2 shard_map.149
  100.3 1.1 collective-permute-start.21
  101.4 1.2 shard_map.146
  102.6 1.0 collective-permute-start.22
  103.6 1.2 shard_map.147
  104.8 3.5 %collective-permute-start.23 = (f32[256,512]{1,0:T(8,128)S(1)}, f32[256,512]{1,0:T(8,128)S(1)}, u32[]{:S(2)}, u32[]{:S(2)}) collective-permute-start(f32[256,512]{1,0:T(8,128)S(1)} %get-tuple-element.86), channel_id=1, source_target_pairs={{0,4},{1,5},{2,6},{3,7},{4,0},{5,1},{6,2},{7,3},{8,12},{9,13},{10,... | collective-permute-start | bytes 1572872 | tf_op jit(solution)/shard_map/ppermute | solution.py:111
  108.3 0.5 collective-permute-start.15
  108.8 2.4 %collective-permute-done.21.refs_6_ = f32[320,512]{1,0:T(8,128)S(1)} collective-permute-done((f32[320,512]{1,0:T(8,128)S(1)}, f32[320,512]{1,0:T(8,128)S(1)}, u32[]{:S(2)}, u32[]{:S(2)}) %collective-permute-start.21) | collective-permute-done | bytes 655392 | tf_op jit(solution)/shard_map/ppermute | solution.py:111
  111.2 0.4 collective-permute-start.24
  111.6 0.3 collective-permute-done.22.refs_7_
  111.9 1.3 collective-permute-start.17
  113.2 1.6 %collective-permute-done.23.refs_8_ = f32[256,512]{1,0:T(8,128)S(1)} collective-permute-done((f32[256,512]{1,0:T(8,128)S(1)}, f32[256,512]{1,0:T(8,128)S(1)}, u32[]{:S(2)}, u32[]{:S(2)}) %collective-permute-start.23) | collective-permute-done | bytes 524320 | tf_op jit(solution)/shard_map/ppermute | solution.py:111
  114.8 0.5 collective-permute-start.26
  115.4 1.4 %collective-permute-done.25.refs_10_ = f32[256,512]{1,0:T(8,128)S(1)} collective-permute-done((f32[256,512]{1,0:T(8,128)S(1)}, f32[256,512]{1,0:T(8,128)S(1)}, u32[]{:S(2)}, u32[]{:S(2)}) %collective-permute-start.25) | collective-permute-done | bytes 524320 | tf_op jit(solution)/shard_map/ppermute | solution.py:96
  116.8 0.7 collective-permute-done.26.refs_11_
  117.5 13.0 %shard_map.150 = (f32[192,768]{1,0:T(8,128)}, f32[256,256]{1,0:T(8,128)}, f32[192,768]{1,0:T(8,128)}, f32[256,256]{1,0:T(8,128)}, f32[192,768]{1,0:T(8,128)}, /*index=5*/f32[256,256]{1,0:T(8,128)}) custom-call(s32[1]{0:T(128)} %bitcast.core_ref, f32[320,512]{1,0:T(8,128)S(1)} %get-tuple-element.76.refs_0_, f32[256,512]{1,0:T(8,128)S(1)} %get-tuple-element.77.refs_1_, ...), custom_call_target="tpu_custom_call" | custom-call | flops 20000000000 | bytes 12000000 | tf_op jit(solution)/shard_map/pallas_call | solution.py:290
  (40 shorter events, 0.4 us)
Async XLA Ops:
  2.3 23.2 %collective-permute-start.1 = (bf16[64,640]{1,0:T(8,128)(2,1)S(1)}, bf16[64,640]{1,0:T(8,128)(2,1)S(1)}, u32[]{:S(2)}, u32[]{:S(2)}) collective-permute-start(bf16[64,640]{1,0:T(8,128)(2,1)S(1)} %pad_maximum_fusion.10), channel_id=1, source_target_pairs={{0,4},{1,5},{2,6},{3,7},{4,0},{5,1},{6,2},{7,3},{8,12},{9,13},{10,... | collective-permute-start | bytes 245768 | tf_op jit(solution)/shard_map/ppermute | solution.py:111
  7.0 18.5 %collective-permute-start.2 = (bf16[64,640]{1,0:T(8,128)(2,1)S(1)}, bf16[64,640]{1,0:T(8,128)(2,1)S(1)}, u32[]{:S(2)}, u32[]{:S(2)}) collective-permute-start(bf16[64,640]{1,0:T(8,128)(2,1)S(1)} %pad_maximum_fusion.11), channel_id=1, source_target_pairs={{0,16},{1,17},{2,18},{3,19},{4,20},{5,21},{6,22},{7,23},{8,24},{9,... | collective-permute-start | bytes 245768 | tf_op jit(solution)/shard_map/ppermute | solution.py:111
  10.3 15.2 %collective-permute-start = (bf16[64,768]{1,0:T(8,128)(2,1)S(1)}, bf16[64,768]{1,0:T(8,128)(2,1)S(1)}, u32[]{:S(2)}, u32[]{:S(2)}) collective-permute-start(bf16[64,768]{1,0:T(8,128)(2,1)S(1)} %pad_maximum_fusion.9), channel_id=1, source_target_pairs={{0,1},{1,0},{2,3},{3,2},{4,5},{5,4},{6,7},{7,6},{8,9},{9,8},{10,11... | collective-permute-start | bytes 294920 | tf_op jit(solution)/shard_map/ppermute | solution.py:111
  13.8 1.6 %copy-start = (bf16[4096,256]{1,0:T(8,128)(2,1)S(1)}, bf16[4096,256]{1,0:T(8,128)(2,1)}, u32[]{:S(2)}) copy-start(bf16[4096,256]{1,0:T(8,128)(2,1)} %grad_kv_ref.1) | copy-start | bytes 6291460
  15.4 1.4 %copy-start.1 = (bf16[4096,192]{0,1:T(8,128)(2,1)S(1)}, bf16[4096,192]{0,1:T(8,128)(2,1)}, u32[]{:S(2)}) copy-start(bf16[4096,192]{0,1:T(8,128)(2,1)} %param.12) | copy-start | bytes 4718596
  25.6 4.9 %collective-permute-start.3 = (bf16[128,768]{1,0:T(8,128)(2,1)S(1)}, bf16[128,768]{1,0:T(8,128)(2,1)S(1)}, u32[]{:S(2)}, u32[]{:S(2)}) collective-permute-start(bf16[128,768]{1,0:T(8,128)(2,1)S(1)} %pad_maximum_fusion.6), channel_id=1, source_target_pairs={{0,3},{1,2},{2,1},{3,0},{4,7},{5,6},{6,5},{7,4},{8,11},{9,10},{10,... | collective-permute-start | bytes 589832 | tf_op jit(solution)/shard_map/ppermute | solution.py:111
  25.7 4.5 %collective-permute-start.4 = (bf16[128,640]{1,0:T(8,128)(2,1)S(1)}, bf16[128,640]{1,0:T(8,128)(2,1)S(1)}, u32[]{:S(2)}, u32[]{:S(2)}) collective-permute-start(bf16[128,640]{1,0:T(8,128)(2,1)S(1)} %get-tuple-element.56), channel_id=1, source_target_pairs={{0,12},{1,13},{2,14},{3,15},{4,8},{5,9},{6,10},{7,11},{8,4},{9,5},... | collective-permute-start | bytes 491528 | tf_op jit(solution)/shard_map/ppermute | solution.py:111
  25.8 4.5 %collective-permute-start.5 = (bf16[128,640]{1,0:T(8,128)(2,1)S(1)}, bf16[128,640]{1,0:T(8,128)(2,1)S(1)}, u32[]{:S(2)}, u32[]{:S(2)}) collective-permute-start(bf16[128,640]{1,0:T(8,128)(2,1)S(1)} %get-tuple-element.57), channel_id=1, source_target_pairs={{0,48},{1,49},{2,50},{3,51},{4,52},{5,53},{6,54},{7,55},{8,56},{9,... | collective-permute-start | bytes 491528 | tf_op jit(solution)/shard_map/ppermute | solution.py:111
  30.6 7.9 %collective-permute-start.6 = (bf16[256,768]{1,0:T(8,128)(2,1)S(1)}, bf16[256,768]{1,0:T(8,128)(2,1)S(1)}, u32[]{:S(2)}, u32[]{:S(2)}) collective-permute-start(bf16[256,768]{1,0:T(8,128)(2,1)S(1)} %pad_maximum_fusion.3), channel_id=1, source_target_pairs={{0,4},{1,5},{2,6},{3,7},{4,0},{5,1},{6,2},{7,3},{8,12},{9,13},{10,... | collective-permute-start | bytes 1179656 | tf_op jit(solution)/shard_map/ppermute | solution.py:111
  30.7 7.2 %collective-permute-start.7 = (bf16[256,640]{1,0:T(8,128)(2,1)S(1)}, bf16[256,640]{1,0:T(8,128)(2,1)S(1)}, u32[]{:S(2)}, u32[]{:S(2)}) collective-permute-start(bf16[256,640]{1,0:T(8,128)(2,1)S(1)} %pad_maximum_fusion.4), channel_id=1, source_target_pairs={{0,16},{1,17},{2,18},{3,19},{4,20},{5,21},{6,22},{7,23},{8,24},{9,... | collective-permute-start | bytes 983048 | tf_op jit(solution)/shard_map/ppermute | solution.py:111
  31.0 7.1 %collective-permute-start.8 = (bf16[256,640]{1,0:T(8,128)(2,1)S(1)}, bf16[256,640]{1,0:T(8,128)(2,1)S(1)}, u32[]{:S(2)}, u32[]{:S(2)}) collective-permute-start(bf16[256,640]{1,0:T(8,128)(2,1)S(1)} %pad_maximum_fusion.5), channel_id=1, source_target_pairs={{0,1},{1,0},{2,3},{3,2},{4,5},{5,4},{6,7},{7,6},{8,9},{9,8},{10,11... | collective-permute-start | bytes 983048 | tf_op jit(solution)/shard_map/ppermute | solution.py:111
  31.3 33.3 %collective-permute-start.18 = (bf16[448,2048]{1,0:T(8,128)(2,1)S(1)}, bf16[448,2048]{1,0:T(8,128)(2,1)S(1)}, u32[]{:S(2)}, u32[]{:S(2)}) collective-permute-start(bf16[448,2048]{1,0:T(8,128)(2,1)S(1)} %get-tuple-element.54), channel_id=1, source_target_pairs={{0,16},{1,17},{2,18},{3,19},{4,20},{5,21},{6,22},{7,23},{8,24},{9,... | collective-permute-start | bytes 5505032 | tf_op jit(solution)/shard_map/ppermute | solution.py:111
  38.6 9.8 %collective-permute-start.11 = (bf16[512,640]{1,0:T(8,128)(2,1)S(1)}, bf16[512,640]{1,0:T(8,128)(2,1)S(1)}, u32[]{:S(2)}, u32[]{:S(2)}) collective-permute-start(bf16[512,640]{1,0:T(8,128)(2,1)S(1)} %pad_maximum_fusion.2), channel_id=1, source_target_pairs={{0,3},{1,2},{2,1},{3,0},{4,7},{5,6},{6,5},{7,4},{8,11},{9,10},{10,... | collective-permute-start | bytes 1966088 | tf_op jit(solution)/shard_map/ppermute | solution.py:111
  39.8 19.7 %collective-permute-start.9 = (bf16[512,768]{1,0:T(8,128)(2,1)S(1)}, bf16[512,768]{1,0:T(8,128)(2,1)S(1)}, u32[]{:S(2)}, u32[]{:S(2)}) collective-permute-start(bf16[512,768]{1,0:T(8,128)(2,1)S(1)} %pad_maximum_fusion), channel_id=1, source_target_pairs={{0,12},{1,13},{2,14},{3,15},{4,8},{5,9},{6,10},{7,11},{8,4},{9,5},... | collective-permute-start | bytes 2359304 | tf_op jit(solution)/shard_map/ppermute | solution.py:111
  40.8 9.8 %collective-permute-start.10 = (bf16[512,640]{1,0:T(8,128)(2,1)S(1)}, bf16[512,640]{1,0:T(8,128)(2,1)S(1)}, u32[]{:S(2)}, u32[]{:S(2)}) collective-permute-start(bf16[512,640]{1,0:T(8,128)(2,1)S(1)} %pad_maximum_fusion.1), channel_id=1, source_target_pairs={{0,48},{1,49},{2,50},{3,51},{4,52},{5,53},{6,54},{7,55},{8,56},{9,... | collective-permute-start | bytes 1966088 | tf_op jit(solution)/shard_map/ppermute | solution.py:111
  40.9 32.3 %collective-permute-start.19 = (bf16[448,2048]{1,0:T(8,128)(2,1)S(1)}, bf16[448,2048]{1,0:T(8,128)(2,1)S(1)}, u32[]{:S(2)}, u32[]{:S(2)}) collective-permute-start(bf16[448,2048]{1,0:T(8,128)(2,1)S(1)} %get-tuple-element.79), channel_id=1, source_target_pairs={{0,1},{1,0},{2,3},{3,2},{4,5},{5,4},{6,7},{7,6},{8,9},{9,8},{10,11... | collective-permute-start | bytes 5505032 | tf_op jit(solution)/shard_map/ppermute | solution.py:111
  48.4 33.8 %collective-permute-start.20 = (bf16[448,2048]{1,0:T(8,128)(2,1)S(1)}, bf16[448,2048]{1,0:T(8,128)(2,1)S(1)}, u32[]{:S(2)}, u32[]{:S(2)}) collective-permute-start(bf16[448,2048]{1,0:T(8,128)(2,1)S(1)} %get-tuple-element.80), channel_id=1, source_target_pairs={{0,4},{1,5},{2,6},{3,7},{4,0},{5,1},{6,2},{7,3},{8,12},{9,13},{10,... | collective-permute-start | bytes 5505032 | tf_op jit(solution)/shard_map/ppermute | solution.py:111
  59.6 39.5 %collective-permute-start.12 = (bf16[1024,768]{1,0:T(8,128)(2,1)S(1)}, bf16[1024,768]{1,0:T(8,128)(2,1)S(1)}, u32[]{:S(2)}, u32[]{:S(2)}) collective-permute-start(bf16[1024,768]{1,0:T(8,128)(2,1)S(1)} %constant_dynamic-update-slice_fusion.refs_0_), channel_id=1, source_target_pairs={{0,48},{1,49},{2,50},{3,51},{4,52},{5,53},{6,54},{7,55},{8,56},{9,... | collective-permute-start | bytes 4718600 | tf_op jit(solution)/shard_map/ppermute | solution.py:111
  59.7 13.5 %copy-start.2 = (f32[1,768,192]{1,2,0:T(8,128)S(1)}, f32[1,768,192]{1,2,0:T(8,128)}, u32[]{:S(2)}) copy-start(f32[1,768,192]{1,2,0:T(8,128)} %param.15) | copy-start | bytes 1769476
  59.8 22.4 %copy-start.4 = (f32[1,256,256]{2,1,0:T(8,128)S(1)}, f32[1,256,256]{2,1,0:T(8,128)}, u32[]{:S(2)}) copy-start(f32[1,256,256]{2,1,0:T(8,128)} %param.16) | copy-start | bytes 786436
  59.9 39.1 %collective-permute-start.14 = (bf16[1024,640]{1,0:T(8,128)(2,1)S(1)}, bf16[1024,640]{1,0:T(8,128)(2,1)S(1)}, u32[]{:S(2)}, u32[]{:S(2)}) collective-permute-start(bf16[1024,640]{1,0:T(8,128)(2,1)S(1)} %constant_dynamic-update-slice_fusion.6.refs_2_), channel_id=1, source_target_pairs={{0,12},{1,13},{2,14},{3,15},{4,8},{5,9},{6,10},{7,11},{8,4},{9,5},... | collective-permute-start | bytes 3932168 | tf_op jit(solution)/shard_map/ppermute | solution.py:111
  64.6 34.5 %collective-permute-start.13 = (bf16[1024,640]{1,0:T(8,128)(2,1)S(1)}, bf16[1024,640]{1,0:T(8,128)(2,1)S(1)}, u32[]{:S(2)}, u32[]{:S(2)}) collective-permute-start(bf16[1024,640]{1,0:T(8,128)(2,1)S(1)} %constant_dynamic-update-slice_fusion.3.refs_1_), channel_id=1, source_target_pairs={{0,3},{1,2},{2,1},{3,0},{4,7},{5,6},{6,5},{7,4},{8,11},{9,10},{10,... | collective-permute-start | bytes 3932168 | tf_op jit(solution)/shard_map/ppermute | solution.py:111
  65.8 33.2 %copy-start.6 = (f32[1,4096]{1,0:T(1,128)S(1)}, f32[1,4096]{1,0:T(1,128)}, u32[]{:S(2)}) copy-start(f32[1,4096]{1,0:T(1,128)} %refs_12_) | copy-start | bytes 49156
  73.3 35.0 %collective-permute-start.28 = (f32[192,768]{1,0:T(8,128)S(1)}, f32[192,768]{1,0:T(8,128)S(1)}, u32[]{:S(2)}, u32[]{:S(2)}) collective-permute-start(f32[192,768]{1,0:T(8,128)S(1)} %bitcast.25), channel_id=1, source_target_pairs={{0,64},{64,0},{1,65},{65,1},{2,66},{66,2},{3,67},{67,3},{4,68},{68... | collective-permute-start | bytes 1769480 | tf_op jit(solution)/shard_map/ppermute | solution.py:96
  82.1 26.1 %collective-permute-start.29 = (f32[256,256]{1,0:T(8,128)S(1)}, f32[256,256]{1,0:T(8,128)S(1)}, u32[]{:S(2)}, u32[]{:S(2)}) collective-permute-start(f32[256,256]{1,0:T(8,128)S(1)} %bitcast.28), channel_id=1, source_target_pairs={{0,64},{64,0},{1,65},{65,1},{2,66},{66,2},{3,67},{67,3},{4,68},{68... | collective-permute-start | bytes 786440 | tf_op jit(solution)/shard_map/ppermute | solution.py:96
  99.0 5.8 %collective-permute-start.27 = (f32[1,4096]{1,0:T(1,128)S(1)}, f32[1,4096]{1,0:T(1,128)S(1)}, u32[]{:S(2)}, u32[]{:S(2)}) collective-permute-start(f32[1,4096]{1,0:T(1,128)S(1)} %copy-done.6), channel_id=1, source_target_pairs={{0,64},{64,0},{1,65},{65,1},{2,66},{66,2},{3,67},{67,3},{4,68},{68... | collective-permute-start | bytes 49160 | tf_op jit(solution)/shard_map/ppermute | solution.py:96
  100.3 10.9 %collective-permute-start.21 = (f32[320,512]{1,0:T(8,128)S(1)}, f32[320,512]{1,0:T(8,128)S(1)}, u32[]{:S(2)}, u32[]{:S(2)}) collective-permute-start(f32[320,512]{1,0:T(8,128)S(1)} %get-tuple-element.84), channel_id=1, source_target_pairs={{0,16},{1,17},{2,18},{3,19},{4,20},{5,21},{6,22},{7,23},{8,24},{9,... | collective-permute-start | bytes 1966088 | tf_op jit(solution)/shard_map/ppermute | solution.py:111
  102.6 9.3 %collective-permute-start.22 = (f32[256,512]{1,0:T(8,128)S(1)}, f32[256,512]{1,0:T(8,128)S(1)}, u32[]{:S(2)}, u32[]{:S(2)}) collective-permute-start(f32[256,512]{1,0:T(8,128)S(1)} %get-tuple-element.85), channel_id=1, source_target_pairs={{0,1},{1,0},{2,3},{3,2},{4,5},{5,4},{6,7},{7,6},{8,9},{9,8},{10,11... | collective-permute-start | bytes 1572872 | tf_op jit(solution)/shard_map/ppermute | solution.py:111
  103.6 13.9 %copy-start.3 = (f32[1,768,192]{1,2,0:T(8,128)S(1)}, f32[1,768,192]{1,2,0:T(8,128)}, u32[]{:S(2)}) copy-start(f32[1,768,192]{1,2,0:T(8,128)} %param.17) | copy-start | bytes 1769476
  103.6 13.9 %copy-start.5 = (f32[1,256,256]{2,1,0:T(8,128)S(1)}, f32[1,256,256]{2,1,0:T(8,128)}, u32[]{:S(2)}) copy-start(f32[1,256,256]{2,1,0:T(8,128)} %param.18) | copy-start | bytes 786436
  104.8 10.1 %collective-permute-start.23 = (f32[256,512]{1,0:T(8,128)S(1)}, f32[256,512]{1,0:T(8,128)S(1)}, u32[]{:S(2)}, u32[]{:S(2)}) collective-permute-start(f32[256,512]{1,0:T(8,128)S(1)} %get-tuple-element.86), channel_id=1, source_target_pairs={{0,4},{1,5},{2,6},{3,7},{4,0},{5,1},{6,2},{7,3},{8,12},{9,13},{10,... | collective-permute-start | bytes 1572872 | tf_op jit(solution)/shard_map/ppermute | solution.py:111
  108.3 6.6 %collective-permute-start.16 = (f32[256,512]{1,0:T(8,128)S(1)}, f32[256,512]{1,0:T(8,128)S(1)}, u32[]{:S(2)}, u32[]{:S(2)}) collective-permute-start(f32[256,512]{1,0:T(8,128)S(1)} %get-tuple-element.77.refs_1_), channel_id=1, source_target_pairs={{0,64},{64,0},{1,65},{65,1},{2,66},{66,2},{3,67},{67,3},{4,68},{68... | collective-permute-start | bytes 1572872 | tf_op jit(solution)/shard_map/ppermute | solution.py:96
  108.3 7.1 %collective-permute-start.15 = (f32[320,512]{1,0:T(8,128)S(1)}, f32[320,512]{1,0:T(8,128)S(1)}, u32[]{:S(2)}, u32[]{:S(2)}) collective-permute-start(f32[320,512]{1,0:T(8,128)S(1)} %get-tuple-element.76.refs_0_), channel_id=1, source_target_pairs={{0,64},{64,0},{1,65},{65,1},{2,66},{66,2},{3,67},{67,3},{4,68},{68... | collective-permute-start | bytes 1966088 | tf_op jit(solution)/shard_map/ppermute | solution.py:96
  111.2 6.3 %collective-permute-start.24 = (f32[320,512]{1,0:T(8,128)S(1)}, f32[320,512]{1,0:T(8,128)S(1)}, u32[]{:S(2)}, u32[]{:S(2)}) collective-permute-start(f32[320,512]{1,0:T(8,128)S(1)} %collective-permute-done.21.refs_6_), channel_id=1, source_target_pairs={{0,64},{64,0},{1,65},{65,1},{2,66},{66,2},{3,67},{67,3},{4,68},{68... | collective-permute-start | bytes 1966088 | tf_op jit(solution)/shard_map/ppermute | solution.py:96
  111.9 3.5 %collective-permute-start.17 = (f32[256,512]{1,0:T(8,128)S(1)}, f32[256,512]{1,0:T(8,128)S(1)}, u32[]{:S(2)}, u32[]{:S(2)}) collective-permute-start(f32[256,512]{1,0:T(8,128)S(1)} %get-tuple-element.78.refs_2_), channel_id=1, source_target_pairs={{0,64},{64,0},{1,65},{65,1},{2,66},{66,2},{3,67},{67,3},{4,68},{68... | collective-permute-start | bytes 1572872 | tf_op jit(solution)/shard_map/ppermute | solution.py:96
  114.8 1.9 %collective-permute-start.25 = (f32[256,512]{1,0:T(8,128)S(1)}, f32[256,512]{1,0:T(8,128)S(1)}, u32[]{:S(2)}, u32[]{:S(2)}) collective-permute-start(f32[256,512]{1,0:T(8,128)S(1)} %collective-permute-done.22.refs_7_), channel_id=1, source_target_pairs={{0,64},{64,0},{1,65},{65,1},{2,66},{66,2},{3,67},{67,3},{4,68},{68... | collective-permute-start | bytes 1572872 | tf_op jit(solution)/shard_map/ppermute | solution.py:96
  114.8 2.7 %collective-permute-start.26 = (f32[256,512]{1,0:T(8,128)S(1)}, f32[256,512]{1,0:T(8,128)S(1)}, u32[]{:S(2)}, u32[]{:S(2)}) collective-permute-start(f32[256,512]{1,0:T(8,128)S(1)} %collective-permute-done.23.refs_8_), channel_id=1, source_target_pairs={{0,64},{64,0},{1,65},{65,1},{2,66},{66,2},{3,67},{67,3},{4,68},{68... | collective-permute-start | bytes 1572872 | tf_op jit(solution)/shard_map/ppermute | solution.py:96

commit v2 on v0

v2 whole, which is shorter than its diff:
```python
import functools
import math

import jax
import jax.numpy as jnp
import numpy as np
from jax import lax
from jax.experimental import pallas as pl
from jax.experimental.pallas import tpu as pltpu
from jax.sharding import PartitionSpec as P

QN = 128
KN = 128
NS_STEPS = 5

coef_a = 3.4445
coef_b = -4.775
coef_c = 2.0315
momentum_rate = 0.95
learn_rate = 0.1
clip_target = 100.0
norm_eps = 1e-07

F32 = jnp.float32
BF16 = jnp.bfloat16

CHIPS = 64
RING = 4
PARTS = 3
LENT = 2
STRIDES = {"z": 16, "y": 4, "x": 1}
AXES = (("xyz", "yzx", "zxy"), ("yzx", "zxy", "xyz"))
HOPS = ((1, 3), (3, 1))
SMEM = pl.BlockSpec(memory_space=pltpu.SMEM)
VMEM = pl.BlockSpec(memory_space=pltpu.VMEM)
MIB = 1024 * 1024


def dot(left, right, left_dim=1, right_dim=0):
    return lax.dot_general(
        left, right, (((left_dim,), (right_dim,)), ((), ())), preferred_element_type=F32
    )


def halves(value):
    high = value.astype(BF16)
    return high, (value - high.astype(F32)).astype(BF16)


def product(left, right):
    (lh, ll), (rh, rl) = left, right
    return dot(lh, rh) + (dot(lh, rl) + dot(ll, rh))


def gram_of(parts):
    high, low = parts
    cross = dot(high, low, 1, 1)
    return dot(high, high, 1, 1) + (cross + cross.T)


def sweep(iterate):
    parts = halves(iterate)
    gram = gram_of(parts)
    gram_parts = halves(gram)
    poly = coef_b * gram + coef_c * product(gram_parts, gram_parts)
    return coef_a * iterate + product(halves(poly), parts)


def normalized(matrix):
    norm = jnp.sqrt(jnp.sum(matrix * matrix, keepdims=True))
    return matrix / (norm + norm_eps)


def swap(value):
    return lax.ppermute(value, "seq", [(0, 1), (1, 0)])


def after(values, earlier):
    return lax.optimization_barrier((values, earlier))[0]


def exchange(value, part, phase, step):
    pairs = []
    for core in range(2):
        stride = STRIDES[AXES[core][part][phase]]
        for chip in range(CHIPS):
            at = chip // stride % RING
            other = chip + ((at ^ HOPS[core][step]) - at) * stride
            pairs.append((core * CHIPS + chip, core * CHIPS + other))
    return lax.ppermute(value, ("seq", "fsdp"), pairs)


def block_orders():
    table = np.zeros((2 * CHIPS, PARTS * CHIPS), np.int32)
    for core in range(2):
        first, second = HOPS[core]
        order = (0, first, second, first ^ second)
        for chip in range(CHIPS):
            for part in range(PARTS):
                for slot in range(CHIPS):
                    chosen = chip
                    for phase in range(3):
                        stride = STRIDES[AXES[core][part][phase]]
                        at = chip // stride % RING
                        turn = order[slot // RING**phase % RING]
                        chosen += ((at ^ turn) - at) * stride
                    table[core * CHIPS + chip, part * CHIPS + slot] = chosen
    return table


def arrange_kernel(first, order_ref, grad_ref, *outs):
    width, tokens = grad_ref.shape
    rows = tokens // CHIPS
    pair = 2 * rows
    left = lax.broadcasted_iota(jnp.int32, (width, pair), 1) < rows

    def joined(one, two):
        turned = []
        for block, half in ((one, 0), (two, 1)):
            tile = grad_ref[:, pl.ds(pl.multiple_of(block // 2 * pair, pair), pair)]
            tile = tile.astype(F32)
            turned.append(jnp.where(block % 2 == half, tile, pltpu.roll(tile, rows, 1)))
        return jnp.where(left, turned[0], turned[1]).astype(BF16)

    for part in range(LENT):
        for slot in (first, first + 2):

            @pl.loop(0, 8)
            def _(at):
                base = part * CHIPS + slot * 16 + at * 2
                lanes = pl.ds(pl.multiple_of((slot // 2 * 8 + at) * pair, pair), pair)
                outs[part][:, lanes] = joined(order_ref[base], order_ref[base + 1])


def arrange(first, order, grad):
    return pl.pallas_call(
        functools.partial(arrange_kernel, first),
        out_shape=(jax.ShapeDtypeStruct((grad.shape[0], grad.shape[1] // 2), BF16),) * LENT,
        in_specs=[SMEM, VMEM],
        out_specs=(VMEM,) * LENT,
        compiler_params=pltpu.CompilerParams(vmem_limit_bytes=12 * MIB),
        cost_estimate=pl.CostEstimate(
            flops=0, bytes_accessed=10_000_000, transcendentals=0
        ),
    )(order, grad)


def line_up_kernel(order_ref, grad_ref, out_ref):
    rows = grad_ref.shape[0] // CHIPS

    @pl.loop(0, CHIPS // RING)
    def _(chunk):
        base = (PARTS - 1) * CHIPS + chunk * RING
        at = [order_ref[base + k] for k in range(RING)]
        spans = [pl.ds(pl.multiple_of(block * rows, rows), rows) for block in at]
        whole = jnp.concatenate([grad_ref[span, :] for span in spans], axis=0)
        lanes = pl.ds(pl.multiple_of(chunk * (RING * rows), RING * rows), RING * rows)
        out_ref[:, lanes] = whole.T


def line_up(order, grad):
    return pl.pallas_call(
        line_up_kernel,
        out_shape=jax.ShapeDtypeStruct(grad.shape[::-1], BF16),
        in_specs=[SMEM, VMEM],
        out_specs=VMEM,
        compiler_params=pltpu.CompilerParams(vmem_limit_bytes=12 * MIB),
        cost_estimate=pl.CostEstimate(
            flops=0, bytes_accessed=10_000_000, transcendentals=0
        ),
    )(order, grad)


def multiply_kernel(slot, count, *refs):
    pieces, grads = refs[:count], refs[count : 2 * count]
    sums, outs = refs[2 * count : -count], refs[-count:]
    for i in range(count):
        span = pieces[i].shape[0]
        term = dot(grads[i][:, slot * span : (slot + 1) * span], pieces[i][...])
        outs[i][...] = term + sums[i][...] if sums else term


def multiply(slot, pieces, grads, sums=()):
    operands = [*pieces, *grads, *sums]
    count = len(pieces)
    return pl.pallas_call(
        functools.partial(multiply_kernel, slot, count),
        out_shape=tuple(
            jax.ShapeDtypeStruct((grad.shape[0], piece.shape[1]), F32)
            for grad, piece in zip(grads, pieces)
        ),
        in_specs=[VMEM] * len(operands),
        out_specs=(VMEM,) * count,
        compiler_params=pltpu.CompilerParams(vmem_limit_bytes=16 * MIB),
        cost_estimate=pl.CostEstimate(
            flops=2_000_000_000, bytes_accessed=8_000_000, transcendentals=0
        ),
    )(*operands)


def clip_factor(peak_ref, peak_other_ref):
    peak = jnp.maximum(
        jnp.max(peak_ref[...], keepdims=True), jnp.max(peak_other_ref[...], keepdims=True)
    )
    return jnp.minimum(1.0, clip_target / peak)


def shares(core_ref, full_ref):
    core, wide = core_ref[0], full_ref.shape[1] // 2
    return tuple(pl.ds(pl.multiple_of(at * wide, 128), wide) for at in (core, 1 - core))


def orthogonalized(full_ref):
    iterate = normalized(full_ref[...])
    for _ in range(NS_STEPS):
        iterate = sweep(iterate)
    full_ref[...] = iterate


def finish_q_kernel(core_ref, *refs):
    packs = [refs[i * LENT : (i + 1) * LENT] for i in range(4)]
    peak_ref, peak_other_ref, mom_ref, mom_other_ref, weight_ref = refs[4 * LENT : -4]
    out_mom_ref, out_upd_ref, out_weight_ref, full_ref = refs[-4:]
    own, other = shares(core_ref, full_ref)
    full_ref[:, own] = momentum_rate * mom_ref[...]
    full_ref[:, other] = momentum_rate * mom_other_ref[...]
    at = 0
    for one, one_swapped, two, two_swapped in zip(*packs):
        wide = one.shape[1]
        full_ref[:, at : at + wide] += (one[...] + one_swapped[...]) + (
            two[...] + two_swapped[...]
        )
        at += wide
    out_mom_ref[...] = full_ref[:, own]
    orthogonalized(full_ref)
    update = (0.2 * math.sqrt(full_ref.shape[1])) * full_ref[:, own]
    out_upd_ref[...] = update
    factor = clip_factor(peak_ref, peak_other_ref)
    rows = lax.broadcasted_iota(jnp.int32, update.shape, 0)
    scale = jnp.where(rows < QN, jnp.sqrt(factor), factor)
    out_weight_ref[...] = (weight_ref[...] - learn_rate * update) * scale


def finish_kv_kernel(core_ref, *refs):
    one, one_swapped, peak_ref, peak_other_ref, mom_ref, mom_other_ref, weight_ref = refs[:7]
    out_mom_ref, out_upd_ref, out_weight_ref, full_ref = refs[7:]
    own, other = shares(core_ref, full_ref)
    full_ref[:, own] = momentum_rate * mom_ref[...].T
    full_ref[:, other] = momentum_rate * mom_other_ref[...].T
    full_ref[...] += one[...] + one_swapped[...]
    out_mom_ref[...] = full_ref[:, own].T
    orthogonalized(full_ref)
    update = ((0.2 * math.sqrt(full_ref.shape[1])) * full_ref[:, own]).T
    out_upd_ref[...] = update
    root = jnp.sqrt(clip_factor(peak_ref, peak_other_ref))
    columns = lax.broadcasted_iota(jnp.int32, update.shape, 1)
    scale = jnp.where(columns < KN, root, 1.0)
    out_weight_ref[...] = (weight_ref[...] - learn_rate * update) * scale


def finish(kernel, full_shape, core, *arrays):
    shape = jax.ShapeDtypeStruct(arrays[-1].shape, F32)
    return pl.pallas_call(
        kernel,
        out_shape=(shape,) * 3,
        in_specs=[SMEM] + [VMEM] * len(arrays),
        out_specs=(VMEM,) * 3,
        scratch_shapes=[pltpu.VMEM(full_shape, F32)],
        compiler_params=pltpu.CompilerParams(vmem_limit_bytes=20 * MIB),
        cost_estimate=pl.CostEstimate(
            flops=10_000_000_000, bytes_accessed=8_000_000, transcendentals=0
        ),
    )(core.reshape(1), *arrays)


def on_device(
    latent_q,
    latent_kv,
    grad_q_heads,
    grad_kv_heads,
    row_peak,
    momentum_q,
    momentum_kv,
    weight_q,
    weight_kv,
):
    core = lax.axis_index("seq")
    device = core * CHIPS + lax.axis_index("fsdp")
    width_q, rank_q = momentum_q.shape[2], latent_q.shape[1]
    width_kv, rank_kv = momentum_kv.shape[2], latent_kv.shape[1]
    unit = rank_q // LENT
    order = lax.dynamic_index_in_dim(jnp.asarray(block_orders()), device, keepdims=False)
    held = [latent_q[:, :unit], latent_q[:, unit:], latent_kv]
    grad_q = grad_q_heads.T
    send = arrange(1, order, grad_q)
    for phase in range(2):
        for step in range(2):
            if phase + step == 1 and step == 1:
                held = after(held, send[0])
            got = [exchange(held[p], p, phase, step) for p in range(PARTS)]
            got = lax.optimization_barrier(got)
            held = [jnp.concatenate([held[p], got[p]], axis=0) for p in range(PARTS)]
    partner = [exchange(send[p], p, 2, 0) for p in range(LENT)]
    third = [exchange(held[p], p, 2, 1) for p in range(PARTS)]
    second = exchange(held[2], 2, 2, 0)
    fourth = exchange(second, 2, 2, 1)
    order, row_peak, mom_q, mom_kv = after(
        (order, row_peak, momentum_q[0].T, momentum_kv[0]), held[0]
    )
    peaks = (row_peak, swap(row_peak))
    moms_q, moms_kv = (mom_q, swap(mom_q)), (mom_kv, swap(mom_kv))
    keep = arrange(0, order, grad_q)
    grad_kv = line_up(order, grad_kv_heads)
    lent = multiply(0, held[:LENT], partner)
    own = multiply(0, held[:LENT], keep)
    own_kv = multiply(0, held[2:], [grad_kv])
    own_kv = multiply(1, [second], [grad_kv], own_kv)
    own_kv = multiply(2, third[2:], [grad_kv], own_kv)
    lent = multiply(1, third[:LENT], partner, lent)
    got = [exchange(lent[p], p, 2, 0) for p in range(LENT)]
    own = multiply(1, third[:LENT], keep, own)
    (own_kv,) = multiply(3, [fourth], [grad_kv], own_kv)
    new_mom_kv, upd_kv, new_weight_kv = finish(
        finish_kv_kernel,
        (width_kv, rank_kv),
        core,
        own_kv,
        swap(own_kv),
        *peaks,
        *moms_kv,
        weight_kv[0],
    )
    got = after(got, new_mom_kv)
    sums = (*own, *[swap(o) for o in own], *got, *[swap(g) for g in got])
    new_mom_q, upd_q, new_weight_q = finish(
        finish_q_kernel, (width_q, rank_q), core, *sums, *peaks, *moms_q, weight_q[0].T
    )
    return (
        new_mom_q.T[None],
        new_mom_kv[None],
        upd_q.T[None],
        upd_kv[None],
        new_weight_q.T[None],
        new_weight_kv[None],
    )


def solution(mesh):
    rows = P("fsdp", "seq", None)
    placed = (
        P(("seq", "fsdp"), None),
        P(("seq", "fsdp"), None),
        P("seq", "fsdp"),
        P("seq", "fsdp"),
        P("fsdp", "seq"),
        rows,
        rows,
        rows,
        rows,
    )
    return jax.shard_map(
        on_device, mesh=mesh, in_specs=placed, out_specs=(rows,) * 6, check_vma=False
    )
```

time: 160 us -> 119 us (0.74)
  waiting for transfers between devices: 111 us -> 37.8 us
  starting transfers between devices: 1.89 us -> 44.4 us
  Pallas kernels: 14.3 us -> 31.4 us
  between operations: 15.5 us -> 1.06 us
  matrix products: 10.8 us -> 0 us
  other arithmetic: 5.45 us -> 0.25 us
  local copies, waits for them, and re-layouts: 1.1 us -> 3.53 us
    all_gather x1 -> x0, waiting for transfers between devices: 110 us -> none  [on_device(): lax.all_gather(jnp.concatenate([latent_q, latent_kv], axis=1), 'fsdp', ax...]
    ppermute x0 -> x21, waiting for transfers between devices: none -> 35.3 us  [exchange(): return lax.ppermute(value, ('seq', 'fsdp'), pairs)]
    ppermute x0 -> x21, starting transfers between devices: none -> 22.9 us  [exchange(): return lax.ppermute(value, ('seq', 'fsdp'), pairs)]
    ppermute x5 -> x8, starting transfers between devices: 1.85 us -> 21.5 us  [swap(): return lax.ppermute(value, 'seq', [(0, 1), (1, 0)])]
    pallas_call x1 -> x13, Pallas kernels: 14.3 us -> 31.4 us  [the longest x2 16.2 us: finish(): pl.pallas_call(kernel, out_shape=(shape,) * 3, in_specs=[SMEM] + [VMEM] *...]
    dot_general x2 -> x0, matrix products: 10.8 us -> none  [dot(): lax.dot_general(left, right, (((left_dim,), (right_dim,)), ((), ())), pre...]
    select_n x2 -> x0, other arithmetic: 3 us -> none  [joined(): jnp.where(core == 0, jnp.concatenate([own, other], axis=axis), jnp.concat...]
  transfers between devices with their start and end apart: 6 -> 29, of which waited for: 2 -> 14; matrix products, arithmetic and copies ran while one was open for 6% -> 1% of each run, Pallas kernels for 0% -> 19%
where the time goes in v2:
time: 119 us; the launch traced here: 118 us
  starting transfers between devices  44.4 us (37%)
  waiting for transfers between devices  37.8 us (32%)
  Pallas kernels  31.4 us (26%)
  local copies, waits for them, and re-layouts  3.53 us (3%)
    ppermute x21, waiting for transfers between devices, exchange(): return lax.ppermute(value, ('seq', 'fsdp'), pairs)  35.3 us
    ppermute x21, starting transfers between devices, exchange(): return lax.ppermute(value, ('seq', 'fsdp'), pairs)  22.9 us
    ppermute x8, starting transfers between devices, swap(): return lax.ppermute(value, 'seq', [(0, 1), (1, 0)])  21.5 us
    pallas_call x2, Pallas kernels, finish(): pl.pallas_call(kernel, out_shape=(shape,) * 3, in_specs=[SMEM] + [VMEM] *...  16.2 us
    pallas_call x2, Pallas kernels, arrange(): pl.pallas_call(functools.partial(arrange_kernel, first), out_shape=(jax.S...  8.27 us
    pallas_call x8, Pallas kernels, multiply(): pl.pallas_call(functools.partial(multiply_kernel, slot, count), out_shape...  4.89 us
    ppermute x8, waiting for transfers between devices, swap(): return lax.ppermute(value, 'seq', [(0, 1), (1, 0)])  2.46 us
  transfers between devices with their start and end apart: 29, of which 14 were waited for; matrix products, arithmetic and copies ran while one was open for 1% of the time, Pallas kernels for 19%

profile of v2, /device:TPU:1, one launch (start us, length us, event | category | flops | bytes accessed | tf_op | source)
XLA Modules:
  0.0 118.4 jit_solution(2476035786667347619)
XLA Ops:
  0.6 1.0 fusion
  1.6 3.6 %collective-permute-start = (bf16[64,768]{1,0:T(8,128)(2,1)S(1)}, bf16[64,768]{1,0:T(8,128)(2,1)S(1)}, u32[]{:S(2)}, u32[]{:S(2)}) collective-permute-start(bf16[64,768]{1,0:T(8,128)(2,1)S(1)} %get-tuple-element.85), channel_id=1, source_target_pairs={{0,1},{1,0},{2,3},{3,2},{4,5},{5,4},{6,7},{7,6},{8,9},{9,8},{10,11... | collective-permute-start | bytes 294920 | tf_op jit(solution)/shard_map/ppermute | solution.py:90
  5.3 3.8 %collective-permute-start.1 = (bf16[64,768]{1,0:T(8,128)(2,1)S(1)}, bf16[64,768]{1,0:T(8,128)(2,1)S(1)}, u32[]{:S(2)}, u32[]{:S(2)}) collective-permute-start(bf16[64,768]{1,0:T(8,128)(2,1)S(1)} %get-tuple-element.84), channel_id=1, source_target_pairs={{0,4},{1,5},{2,6},{3,7},{4,0},{5,1},{6,2},{7,3},{8,12},{9,13},{10,... | collective-permute-start | bytes 294920 | tf_op jit(solution)/shard_map/ppermute | solution.py:90
  9.0 2.5 %collective-permute-start.2 = (bf16[64,512]{1,0:T(8,128)(2,1)}, bf16[64,512]{1,0:T(8,128)(2,1)S(1)}, u32[]{:S(2)}, u32[]{:S(2)}) collective-permute-start(bf16[64,512]{1,0:T(8,128)(2,1)} %param.11), channel_id=1, source_target_pairs={{0,16},{1,17},{2,18},{3,19},{4,20},{5,21},{6,22},{7,23},{8,24},{9,... | collective-permute-start | bytes 196616 | tf_op jit(solution)/shard_map/ppermute | solution.py:90
  11.5 0.7 constant_dynamic-slice_fusion
  12.2 1.4 %copy-done = bf16[4096,192]{0,1:T(8,128)(2,1)S(1)} copy-done((bf16[4096,192]{0,1:T(8,128)(2,1)S(1)}, bf16[4096,192]{0,1:T(8,128)(2,1)}, u32[]{:S(2)}) %copy-start) | copy-done | bytes 1572888
  13.6 4.1 %shard_map.145 = (bf16[192,2048]{1,0:T(8,128)(2,1)S(1)}, bf16[192,2048]{1,0:T(8,128)(2,1)S(1)}) custom-call(s32[192]{0:T(256)S(1)} %bitcast.25, bf16[192,4096]{1,0:T(8,128)(2,1)S(1)} %bitcast.23), custom_call_target="tpu_custom_call" | custom-call | bytes 10000000 | tf_op jit(solution)/shard_map/pallas_call | solution.py:136
  17.9 0.1 collective-permute-start.3
  18.0 0.1 collective-permute-start.4
  18.0 0.1 collective-permute-start.5
  18.1 4.1 %collective-permute-done.5 = bf16[128,512]{1,0:T(8,128)(2,1)S(1)} collective-permute-done((bf16[128,512]{1,0:T(8,128)(2,1)S(1)}, bf16[128,512]{1,0:T(8,128)(2,1)S(1)}, u32[]{:S(2)}, u32[]{:S(2)}) %collective-permute-start.5) | collective-permute-done | bytes 131104 | tf_op jit(solution)/shard_map/ppermute | solution.py:90
  22.2 0.5 collective-permute-done.3
  22.8 0.1 collective-permute-done.4
  22.9 0.3 collective-permute-start.7
  23.2 0.1 collective-permute-start.6
  23.3 0.6 collective-permute-start.8
  23.9 5.9 %collective-permute-done.8 = bf16[256,512]{1,0:T(8,128)(2,1)S(1)} collective-permute-done((bf16[256,512]{1,0:T(8,128)(2,1)S(1)}, bf16[256,512]{1,0:T(8,128)(2,1)S(1)}, u32[]{:S(2)}, u32[]{:S(2)}) %collective-permute-start.8) | collective-permute-done | bytes 262176 | tf_op jit(solution)/shard_map/ppermute | solution.py:90
  29.8 1.0 collective-permute-done.7
  30.8 0.3 collective-permute-done.6
  31.1 0.1 pad_maximum_fusion.1
  31.2 0.1 collective-permute-start.10
  31.3 0.1 pad_maximum_fusion
  31.3 0.5 collective-permute-start.9
  31.9 1.5 %collective-permute-start.11 = (bf16[512,512]{1,0:T(8,128)(2,1)S(1)}, bf16[512,512]{1,0:T(8,128)(2,1)S(1)}, u32[]{:S(2)}, u32[]{:S(2)}) collective-permute-start(bf16[512,512]{1,0:T(8,128)(2,1)S(1)} %pad_maximum_fusion.2), channel_id=1, source_target_pairs={{0,3},{1,2},{2,1},{3,0},{4,7},{5,6},{6,5},{7,4},{8,11},{9,10},{10,... | collective-permute-start | bytes 1572872 | tf_op jit(solution)/shard_map/ppermute | solution.py:90
  33.4 6.9 %collective-permute-done.11 = bf16[512,512]{1,0:T(8,128)(2,1)S(1)} collective-permute-done((bf16[512,512]{1,0:T(8,128)(2,1)S(1)}, bf16[512,512]{1,0:T(8,128)(2,1)S(1)}, u32[]{:S(2)}, u32[]{:S(2)}) %collective-permute-start.11) | collective-permute-done | bytes 524320 | tf_op jit(solution)/shard_map/ppermute | solution.py:90
  40.3 2.1 %collective-permute-done.10 = bf16[512,768]{1,0:T(8,128)(2,1)S(1)} collective-permute-done((bf16[512,768]{1,0:T(8,128)(2,1)S(1)}, bf16[512,768]{1,0:T(8,128)(2,1)S(1)}, u32[]{:S(2)}, u32[]{:S(2)}) %collective-permute-start.10) | collective-permute-done | bytes 786464 | tf_op jit(solution)/shard_map/ppermute | solution.py:90
  42.4 0.2 collective-permute-done.9
  42.6 1.5 %collective-permute-start.20 = (bf16[1024,512]{1,0:T(8,128)(2,1)S(1)}, bf16[1024,512]{1,0:T(8,128)(2,1)S(1)}, u32[]{:S(2)}, u32[]{:S(2)}) collective-permute-start(bf16[1024,512]{1,0:T(8,128)(2,1)S(1)} %constant_dynamic-update-slice_fusion.8.refs_0_), channel_id=1, source_target_pairs={{0,4},{1,5},{2,6},{3,7},{4,0},{5,1},{6,2},{7,3},{8,12},{9,13},{10,... | collective-permute-start | bytes 3145736 | tf_op jit(solution)/shard_map/ppermute | solution.py:90
  44.1 0.1 collective-permute-start.22
  44.3 0.0 copy-start.2
  44.3 0.1 constant_dynamic-update-slice_fusion.4.refs_1_
  44.4 1.1 collective-permute-start.13
  45.5 0.1 constant_dynamic-update-slice_fusion.refs_0_
  45.5 1.0 collective-permute-start.12
  46.5 11.5 %collective-permute-done.20.refs_0_ = bf16[1024,512]{1,0:T(8,128)(2,1)S(1)} collective-permute-done((bf16[1024,512]{1,0:T(8,128)(2,1)S(1)}, bf16[1024,512]{1,0:T(8,128)(2,1)S(1)}, u32[]{:S(2)}, u32[]{:S(2)}) %collective-permute-start.20) | collective-permute-done | bytes 1048608 | tf_op jit(solution)/shard_map/ppermute | solution.py:90
  58.0 1.3 %collective-permute-start.21 = (bf16[1024,512]{1,0:T(8,128)(2,1)S(1)}, bf16[1024,512]{1,0:T(8,128)(2,1)S(1)}, u32[]{:S(2)}, u32[]{:S(2)}) collective-permute-start(bf16[1024,512]{1,0:T(8,128)(2,1)S(1)} %collective-permute-done.20.refs_0_), channel_id=1, source_target_pairs={{0,12},{1,13},{2,14},{3,15},{4,8},{5,9},{6,10},{7,11},{8,4},{9,5},... | collective-permute-start | bytes 3145736 | tf_op jit(solution)/shard_map/ppermute | solution.py:90
  59.3 1.2 collective-permute-start.16
  60.5 2.0 %shard_map.151.refs_1_ = bf16[256,4096]{1,0:T(8,128)(2,1)S(1)} custom-call(s32[192]{0:T(256)S(1)} %bitcast.26, bf16[4096,256]{1,0:T(8,128)(2,1)S(1)} %copy-done.2), custom_call_target="tpu_custom_call" | custom-call | bytes 10000000 | tf_op jit(solution)/shard_map/pallas_call | solution.py:162
  62.5 0.9 collective-permute-start.17
  63.4 0.4 shard_map.152.refs_2_
  63.8 0.1 copy-done.1
  63.9 4.1 %shard_map.146 = (bf16[192,2048]{1,0:T(8,128)(2,1)S(1)}, bf16[192,2048]{1,0:T(8,128)(2,1)S(1)}) custom-call(s32[192]{0:T(256)S(1)} %bitcast.27, bf16[192,4096]{1,0:T(8,128)(2,1)S(1)} %bitcast.24), custom_call_target="tpu_custom_call" | custom-call | bytes 10000000 | tf_op jit(solution)/shard_map/pallas_call | solution.py:136
  68.0 0.8 shard_map.147
  68.8 0.4 shard_map.153.refs_2_
  69.3 0.4 shard_map.154.refs_2_
  69.7 2.2 %collective-permute-done.21.refs_0_ = bf16[1024,512]{1,0:T(8,128)(2,1)S(1)} collective-permute-done((bf16[1024,512]{1,0:T(8,128)(2,1)S(1)}, bf16[1024,512]{1,0:T(8,128)(2,1)S(1)}, u32[]{:S(2)}, u32[]{:S(2)}) %collective-permute-start.21) | collective-permute-done | bytes 1048608 | tf_op jit(solution)/shard_map/ppermute | solution.py:90
  71.9 19.7 %collective-permute-start.25 = (f32[256,256]{1,0:T(8,128)S(1)}, f32[256,256]{1,0:T(8,128)S(1)}, u32[]{:S(2)}, u32[]{:S(2)}) collective-permute-start(f32[256,256]{1,0:T(8,128)S(1)} %bitcast.31), channel_id=1, source_target_pairs={{0,64},{64,0},{1,65},{65,1},{2,66},{66,2},{3,67},{67,3},{4,68},{68... | collective-permute-start | bytes 786440 | tf_op jit(solution)/shard_map/ppermute | solution.py:75
  91.6 0.4 shard_map.155.refs_0_
  92.1 0.1 collective-permute-start.24
  92.2 0.5 collective-permute-start.23
  92.7 0.8 shard_map.149
  93.5 0.2 collective-permute-start.28
  93.7 0.8 shard_map.150
  94.5 1.0 collective-permute-start.18
  95.5 0.8 shard_map.148
  96.4 1.7 %collective-permute-start.19 = (f32[192,768]{1,0:T(8,128)S(1)}, f32[192,768]{1,0:T(8,128)S(1)}, u32[]{:S(2)}, u32[]{:S(2)}) collective-permute-start(f32[192,768]{1,0:T(8,128)S(1)} %get-tuple-element.71), channel_id=1, source_target_pairs={{0,1},{1,0},{2,3},{3,2},{4,5},{5,4},{6,7},{7,6},{8,9},{9,8},{10,11... | collective-permute-start | bytes 1769480 | tf_op jit(solution)/shard_map/ppermute | solution.py:90
  98.1 0.5 collective-permute-start.15
  98.6 7.2 %shard_map.156 = (f32[256,256]{1,0:T(8,128)}, f32[256,256]{1,0:T(8,128)}, f32[256,256]{1,0:T(8,128)}) custom-call(s32[1]{0:T(128)} %bitcast.core_ref, f32[256,512]{1,0:T(8,128)S(1)} %shard_map.155.refs_0_, f32[256,512]{1,0:T(8,128)S(1)} %collective-permute-done.23.refs_1_, f32[1,4096]{1,0:T(1,128)S(1)} %copy-done.7, ...), custom_call_target="tpu_custom_call" | custom-call | flops 10000000000 | bytes 8000000 | tf_op jit(solution)/shard_map/pallas_call | solution.py:263
  105.8 0.6 collective-permute-done.19.refs_5_
  106.4 0.5 collective-permute-start.26
  106.9 0.0 collective-permute-start.27
  106.9 1.6 %collective-permute-done.26.refs_6_ = f32[192,768]{1,0:T(8,128)S(1)} collective-permute-done((f32[192,768]{1,0:T(8,128)S(1)}, f32[192,768]{1,0:T(8,128)S(1)}, u32[]{:S(2)}, u32[]{:S(2)}) %collective-permute-start.26) | collective-permute-done | bytes 589856 | tf_op jit(solution)/shard_map/ppermute | solution.py:75
  108.5 0.8 collective-permute-done.27.refs_7_
  109.4 9.1 %shard_map.157 = (f32[192,768]{1,0:T(8,128)}, f32[192,768]{1,0:T(8,128)}, f32[192,768]{1,0:T(8,128)}) custom-call(s32[1]{0:T(128)} %bitcast.core_ref, f32[192,768]{1,0:T(8,128)S(1)} %get-tuple-element.65.refs_0_, f32[192,768]{1,0:T(8,128)S(1)} %get-tuple-element.66.refs_1_, f32[192,768]{1,0:T(8,128)S(1)} %collective-permute-done.14.refs_2_, ...), custom_call_target="tpu_custom_call" | custom-call | flops 10000000000 | bytes 8000000 | tf_op jit(solution)/shard_map/pallas_call | solution.py:263
  (47 shorter events, 0.4 us)
Async XLA Ops:
  0.6 17.2 %copy-start.8 = (bf16[64,512]{1,0:T(8,128)(2,1)S(1)}, bf16[64,512]{1,0:T(8,128)(2,1)}, u32[]{:S(2)}) copy-start(bf16[64,512]{1,0:T(8,128)(2,1)} %param.11) | copy-start | bytes 196612
  1.6 16.1 %collective-permute-start = (bf16[64,768]{1,0:T(8,128)(2,1)S(1)}, bf16[64,768]{1,0:T(8,128)(2,1)S(1)}, u32[]{:S(2)}, u32[]{:S(2)}) collective-permute-start(bf16[64,768]{1,0:T(8,128)(2,1)S(1)} %get-tuple-element.85), channel_id=1, source_target_pairs={{0,1},{1,0},{2,3},{3,2},{4,5},{5,4},{6,7},{7,6},{8,9},{9,8},{10,11... | collective-permute-start | bytes 294920 | tf_op jit(solution)/shard_map/ppermute | solution.py:90
  5.3 12.5 %collective-permute-start.1 = (bf16[64,768]{1,0:T(8,128)(2,1)S(1)}, bf16[64,768]{1,0:T(8,128)(2,1)S(1)}, u32[]{:S(2)}, u32[]{:S(2)}) collective-permute-start(bf16[64,768]{1,0:T(8,128)(2,1)S(1)} %get-tuple-element.84), channel_id=1, source_target_pairs={{0,4},{1,5},{2,6},{3,7},{4,0},{5,1},{6,2},{7,3},{8,12},{9,13},{10,... | collective-permute-start | bytes 294920 | tf_op jit(solution)/shard_map/ppermute | solution.py:90
  9.0 8.7 %collective-permute-start.2 = (bf16[64,512]{1,0:T(8,128)(2,1)}, bf16[64,512]{1,0:T(8,128)(2,1)S(1)}, u32[]{:S(2)}, u32[]{:S(2)}) collective-permute-start(bf16[64,512]{1,0:T(8,128)(2,1)} %param.11), channel_id=1, source_target_pairs={{0,16},{1,17},{2,18},{3,19},{4,20},{5,21},{6,22},{7,23},{8,24},{9,... | collective-permute-start | bytes 196616 | tf_op jit(solution)/shard_map/ppermute | solution.py:90
  12.2 1.4 %copy-start = (bf16[4096,192]{0,1:T(8,128)(2,1)S(1)}, bf16[4096,192]{0,1:T(8,128)(2,1)}, u32[]{:S(2)}) copy-start(bf16[4096,192]{0,1:T(8,128)(2,1)} %param.12) | copy-start | bytes 4718596
  17.9 4.9 %collective-permute-start.3 = (bf16[128,768]{1,0:T(8,128)(2,1)S(1)}, bf16[128,768]{1,0:T(8,128)(2,1)S(1)}, u32[]{:S(2)}, u32[]{:S(2)}) collective-permute-start(bf16[128,768]{1,0:T(8,128)(2,1)S(1)} %get-tuple-element.49), channel_id=1, source_target_pairs={{0,3},{1,2},{2,1},{3,0},{4,7},{5,6},{6,5},{7,4},{8,11},{9,10},{10,... | collective-permute-start | bytes 589832 | tf_op jit(solution)/shard_map/ppermute | solution.py:90
  18.0 4.9 %collective-permute-start.4 = (bf16[128,768]{1,0:T(8,128)(2,1)S(1)}, bf16[128,768]{1,0:T(8,128)(2,1)S(1)}, u32[]{:S(2)}, u32[]{:S(2)}) collective-permute-start(bf16[128,768]{1,0:T(8,128)(2,1)S(1)} %get-tuple-element.50), channel_id=1, source_target_pairs={{0,12},{1,13},{2,14},{3,15},{4,8},{5,9},{6,10},{7,11},{8,4},{9,5},... | collective-permute-start | bytes 589832 | tf_op jit(solution)/shard_map/ppermute | solution.py:90
  18.0 4.2 %collective-permute-start.5 = (bf16[128,512]{1,0:T(8,128)(2,1)S(1)}, bf16[128,512]{1,0:T(8,128)(2,1)S(1)}, u32[]{:S(2)}, u32[]{:S(2)}) collective-permute-start(bf16[128,512]{1,0:T(8,128)(2,1)S(1)} %pad_maximum_fusion.8), channel_id=1, source_target_pairs={{0,48},{1,49},{2,50},{3,51},{4,52},{5,53},{6,54},{7,55},{8,56},{9,... | collective-permute-start | bytes 393224 | tf_op jit(solution)/shard_map/ppermute | solution.py:90
  22.9 7.9 %collective-permute-start.7 = (bf16[256,768]{1,0:T(8,128)(2,1)S(1)}, bf16[256,768]{1,0:T(8,128)(2,1)S(1)}, u32[]{:S(2)}, u32[]{:S(2)}) collective-permute-start(bf16[256,768]{1,0:T(8,128)(2,1)S(1)} %pad_maximum_fusion.4), channel_id=1, source_target_pairs={{0,16},{1,17},{2,18},{3,19},{4,20},{5,21},{6,22},{7,23},{8,24},{9,... | collective-permute-start | bytes 1179656 | tf_op jit(solution)/shard_map/ppermute | solution.py:90
  23.2 7.9 %collective-permute-start.6 = (bf16[256,768]{1,0:T(8,128)(2,1)S(1)}, bf16[256,768]{1,0:T(8,128)(2,1)S(1)}, u32[]{:S(2)}, u32[]{:S(2)}) collective-permute-start(bf16[256,768]{1,0:T(8,128)(2,1)S(1)} %pad_maximum_fusion.3), channel_id=1, source_target_pairs={{0,4},{1,5},{2,6},{3,7},{4,0},{5,1},{6,2},{7,3},{8,12},{9,13},{10,... | collective-permute-start | bytes 1179656 | tf_op jit(solution)/shard_map/ppermute | solution.py:90
  23.3 6.5 %collective-permute-start.8 = (bf16[256,512]{1,0:T(8,128)(2,1)S(1)}, bf16[256,512]{1,0:T(8,128)(2,1)S(1)}, u32[]{:S(2)}, u32[]{:S(2)}) collective-permute-start(bf16[256,512]{1,0:T(8,128)(2,1)S(1)} %pad_maximum_fusion.5), channel_id=1, source_target_pairs={{0,1},{1,0},{2,3},{3,2},{4,5},{5,4},{6,7},{7,6},{8,9},{9,8},{10,11... | collective-permute-start | bytes 786440 | tf_op jit(solution)/shard_map/ppermute | solution.py:90
  31.2 11.2 %collective-permute-start.10 = (bf16[512,768]{1,0:T(8,128)(2,1)S(1)}, bf16[512,768]{1,0:T(8,128)(2,1)S(1)}, u32[]{:S(2)}, u32[]{:S(2)}) collective-permute-start(bf16[512,768]{1,0:T(8,128)(2,1)S(1)} %pad_maximum_fusion.1), channel_id=1, source_target_pairs={{0,48},{1,49},{2,50},{3,51},{4,52},{5,53},{6,54},{7,55},{8,56},{9,... | collective-permute-start | bytes 2359304 | tf_op jit(solution)/shard_map/ppermute | solution.py:90
  31.3 11.2 %collective-permute-start.9 = (bf16[512,768]{1,0:T(8,128)(2,1)S(1)}, bf16[512,768]{1,0:T(8,128)(2,1)S(1)}, u32[]{:S(2)}, u32[]{:S(2)}) collective-permute-start(bf16[512,768]{1,0:T(8,128)(2,1)S(1)} %pad_maximum_fusion), channel_id=1, source_target_pairs={{0,12},{1,13},{2,14},{3,15},{4,8},{5,9},{6,10},{7,11},{8,4},{9,5},... | collective-permute-start | bytes 2359304 | tf_op jit(solution)/shard_map/ppermute | solution.py:90
  31.9 8.4 %collective-permute-start.11 = (bf16[512,512]{1,0:T(8,128)(2,1)S(1)}, bf16[512,512]{1,0:T(8,128)(2,1)S(1)}, u32[]{:S(2)}, u32[]{:S(2)}) collective-permute-start(bf16[512,512]{1,0:T(8,128)(2,1)S(1)} %pad_maximum_fusion.2), channel_id=1, source_target_pairs={{0,3},{1,2},{2,1},{3,0},{4,7},{5,6},{6,5},{7,4},{8,11},{9,10},{10,... | collective-permute-start | bytes 1572872 | tf_op jit(solution)/shard_map/ppermute | solution.py:90
  42.6 15.4 %collective-permute-start.20 = (bf16[1024,512]{1,0:T(8,128)(2,1)S(1)}, bf16[1024,512]{1,0:T(8,128)(2,1)S(1)}, u32[]{:S(2)}, u32[]{:S(2)}) collective-permute-start(bf16[1024,512]{1,0:T(8,128)(2,1)S(1)} %constant_dynamic-update-slice_fusion.8.refs_0_), channel_id=1, source_target_pairs={{0,4},{1,5},{2,6},{3,7},{4,0},{5,1},{6,2},{7,3},{8,12},{9,13},{10,... | collective-permute-start | bytes 3145736 | tf_op jit(solution)/shard_map/ppermute | solution.py:90
  44.1 18.4 %collective-permute-start.22 = (bf16[1024,512]{1,0:T(8,128)(2,1)S(1)}, bf16[1024,512]{1,0:T(8,128)(2,1)S(1)}, u32[]{:S(2)}, u32[]{:S(2)}) collective-permute-start(bf16[1024,512]{1,0:T(8,128)(2,1)S(1)} %constant_dynamic-update-slice_fusion.8.refs_0_), channel_id=1, source_target_pairs={{0,12},{1,13},{2,14},{3,15},{4,8},{5,9},{6,10},{7,11},{8,4},{9,5},... | collective-permute-start | bytes 3145736 | tf_op jit(solution)/shard_map/ppermute | solution.py:90
  44.3 16.2 %copy-start.2 = (bf16[4096,256]{1,0:T(8,128)(2,1)S(1)}, bf16[4096,256]{1,0:T(8,128)(2,1)}, u32[]{:S(2)}) copy-start(bf16[4096,256]{1,0:T(8,128)(2,1)} %grad_ref.1) | copy-start | bytes 6291460
  44.4 49.2 %collective-permute-start.13 = (bf16[1024,768]{1,0:T(8,128)(2,1)S(1)}, bf16[1024,768]{1,0:T(8,128)(2,1)S(1)}, u32[]{:S(2)}, u32[]{:S(2)}) collective-permute-start(bf16[1024,768]{1,0:T(8,128)(2,1)S(1)} %constant_dynamic-update-slice_fusion.4.refs_1_), channel_id=1, source_target_pairs={{0,3},{1,2},{2,1},{3,0},{4,7},{5,6},{6,5},{7,4},{8,11},{9,10},{10,... | collective-permute-start | bytes 4718600 | tf_op jit(solution)/shard_map/ppermute | solution.py:90
  45.5 48.2 %collective-permute-start.12 = (bf16[1024,768]{1,0:T(8,128)(2,1)S(1)}, bf16[1024,768]{1,0:T(8,128)(2,1)S(1)}, u32[]{:S(2)}, u32[]{:S(2)}) collective-permute-start(bf16[1024,768]{1,0:T(8,128)(2,1)S(1)} %constant_dynamic-update-slice_fusion.refs_0_), channel_id=1, source_target_pairs={{0,48},{1,49},{2,50},{3,51},{4,52},{5,53},{6,54},{7,55},{8,56},{9,... | collective-permute-start | bytes 4718600 | tf_op jit(solution)/shard_map/ppermute | solution.py:90
  58.0 13.9 %collective-permute-start.21 = (bf16[1024,512]{1,0:T(8,128)(2,1)S(1)}, bf16[1024,512]{1,0:T(8,128)(2,1)S(1)}, u32[]{:S(2)}, u32[]{:S(2)}) collective-permute-start(bf16[1024,512]{1,0:T(8,128)(2,1)S(1)} %collective-permute-done.20.refs_0_), channel_id=1, source_target_pairs={{0,12},{1,13},{2,14},{3,15},{4,8},{5,9},{6,10},{7,11},{8,4},{9,5},... | collective-permute-start | bytes 3145736 | tf_op jit(solution)/shard_map/ppermute | solution.py:90
  59.3 32.8 %collective-permute-start.16 = (bf16[192,2048]{1,0:T(8,128)(2,1)S(1)}, bf16[192,2048]{1,0:T(8,128)(2,1)S(1)}, u32[]{:S(2)}, u32[]{:S(2)}) collective-permute-start(bf16[192,2048]{1,0:T(8,128)(2,1)S(1)} %get-tuple-element.48), channel_id=1, source_target_pairs={{0,16},{1,17},{2,18},{3,19},{4,20},{5,21},{6,22},{7,23},{8,24},{9,... | collective-permute-start | bytes 2359304 | tf_op jit(solution)/shard_map/ppermute | solution.py:90
  62.5 1.4 %copy-start.1 = (bf16[4096,192]{0,1:T(8,128)(2,1)S(1)}, bf16[4096,192]{0,1:T(8,128)(2,1)}, u32[]{:S(2)}) copy-start(bf16[4096,192]{0,1:T(8,128)(2,1)} %param.12) | copy-start | bytes 4718596
  62.5 29.7 %collective-permute-start.17 = (bf16[192,2048]{1,0:T(8,128)(2,1)S(1)}, bf16[192,2048]{1,0:T(8,128)(2,1)S(1)}, u32[]{:S(2)}, u32[]{:S(2)}) collective-permute-start(bf16[192,2048]{1,0:T(8,128)(2,1)S(1)} %get-tuple-element.67), channel_id=1, source_target_pairs={{0,1},{1,0},{2,3},{3,2},{4,5},{5,4},{6,7},{7,6},{8,9},{9,8},{10,11... | collective-permute-start | bytes 2359304 | tf_op jit(solution)/shard_map/ppermute | solution.py:90
  69.3 2.6 %copy-start.5 = (f32[1,256,256]{2,1,0:T(8,128)S(1)}, f32[1,256,256]{2,1,0:T(8,128)}, u32[]{:S(2)}) copy-start(f32[1,256,256]{2,1,0:T(8,128)} %param.16) | copy-start | bytes 786436
  69.7 22.4 %copy-start.7 = (f32[1,4096]{1,0:T(1,128)S(1)}, f32[1,4096]{1,0:T(1,128)}, u32[]{:S(2)}) copy-start(f32[1,4096]{1,0:T(1,128)} %refs_8_) | copy-start | bytes 49156
  71.9 26.2 %collective-permute-start.25 = (f32[256,256]{1,0:T(8,128)S(1)}, f32[256,256]{1,0:T(8,128)S(1)}, u32[]{:S(2)}, u32[]{:S(2)}) collective-permute-start(f32[256,256]{1,0:T(8,128)S(1)} %bitcast.31), channel_id=1, source_target_pairs={{0,64},{64,0},{1,65},{65,1},{2,66},{66,2},{3,67},{67,3},{4,68},{68... | collective-permute-start | bytes 786440 | tf_op jit(solution)/shard_map/ppermute | solution.py:75
  92.1 1.4 %copy-start.3 = (f32[1,768,192]{1,2,0:T(8,128)S(1)}, f32[1,768,192]{1,2,0:T(8,128)}, u32[]{:S(2)}) copy-start(f32[1,768,192]{1,2,0:T(8,128)} %param.15) | copy-start | bytes 1769476
  92.1 4.2 %collective-permute-start.24 = (f32[1,4096]{1,0:T(1,128)S(1)}, f32[1,4096]{1,0:T(1,128)S(1)}, u32[]{:S(2)}, u32[]{:S(2)}) collective-permute-start(f32[1,4096]{1,0:T(1,128)S(1)} %copy-done.7), channel_id=1, source_target_pairs={{0,64},{64,0},{1,65},{65,1},{2,66},{66,2},{3,67},{67,3},{4,68},{68... | collective-permute-start | bytes 49160 | tf_op jit(solution)/shard_map/ppermute | solution.py:75
  92.2 5.9 %collective-permute-start.23 = (f32[256,512]{1,0:T(8,128)S(1)}, f32[256,512]{1,0:T(8,128)S(1)}, u32[]{:S(2)}, u32[]{:S(2)}) collective-permute-start(f32[256,512]{1,0:T(8,128)S(1)} %shard_map.155.refs_0_), channel_id=1, source_target_pairs={{0,64},{64,0},{1,65},{65,1},{2,66},{66,2},{3,67},{67,3},{4,68},{68... | collective-permute-start | bytes 1572872 | tf_op jit(solution)/shard_map/ppermute | solution.py:75
  93.5 13.4 %collective-permute-start.28 = (f32[192,768]{1,0:T(8,128)S(1)}, f32[192,768]{1,0:T(8,128)S(1)}, u32[]{:S(2)}, u32[]{:S(2)}) collective-permute-start(f32[192,768]{1,0:T(8,128)S(1)} %bitcast.28), channel_id=1, source_target_pairs={{0,64},{64,0},{1,65},{65,1},{2,66},{66,2},{3,67},{67,3},{4,68},{68... | collective-permute-start | bytes 1769480 | tf_op jit(solution)/shard_map/ppermute | solution.py:75
  94.5 11.3 %collective-permute-start.18 = (f32[192,768]{1,0:T(8,128)S(1)}, f32[192,768]{1,0:T(8,128)S(1)}, u32[]{:S(2)}, u32[]{:S(2)}) collective-permute-start(f32[192,768]{1,0:T(8,128)S(1)} %get-tuple-element.70), channel_id=1, source_target_pairs={{0,16},{1,17},{2,18},{3,19},{4,20},{5,21},{6,22},{7,23},{8,24},{9,... | collective-permute-start | bytes 1769480 | tf_op jit(solution)/shard_map/ppermute | solution.py:90
  95.5 3.0 %copy-start.6 = (f32[1,256,256]{2,1,0:T(8,128)S(1)}, f32[1,256,256]{2,1,0:T(8,128)}, u32[]{:S(2)}) copy-start(f32[1,256,256]{2,1,0:T(8,128)} %param.18) | copy-start | bytes 786436
  96.4 10.0 %collective-permute-start.19 = (f32[192,768]{1,0:T(8,128)S(1)}, f32[192,768]{1,0:T(8,128)S(1)}, u32[]{:S(2)}, u32[]{:S(2)}) collective-permute-start(f32[192,768]{1,0:T(8,128)S(1)} %get-tuple-element.71), channel_id=1, source_target_pairs={{0,1},{1,0},{2,3},{3,2},{4,5},{5,4},{6,7},{7,6},{8,9},{9,8},{10,11... | collective-permute-start | bytes 1769480 | tf_op jit(solution)/shard_map/ppermute | solution.py:90
  98.1 8.8 %collective-permute-start.14 = (f32[192,768]{1,0:T(8,128)S(1)}, f32[192,768]{1,0:T(8,128)S(1)}, u32[]{:S(2)}, u32[]{:S(2)}) collective-permute-start(f32[192,768]{1,0:T(8,128)S(1)} %get-tuple-element.65.refs_0_), channel_id=1, source_target_pairs={{0,64},{64,0},{1,65},{65,1},{2,66},{66,2},{3,67},{67,3},{4,68},{68... | collective-permute-start | bytes 1769480 | tf_op jit(solution)/shard_map/ppermute | solution.py:75
  98.1 8.8 %collective-permute-start.15 = (f32[192,768]{1,0:T(8,128)S(1)}, f32[192,768]{1,0:T(8,128)S(1)}, u32[]{:S(2)}, u32[]{:S(2)}) collective-permute-start(f32[192,768]{1,0:T(8,128)S(1)} %get-tuple-element.66.refs_1_), channel_id=1, source_target_pairs={{0,64},{64,0},{1,65},{65,1},{2,66},{66,2},{3,67},{67,3},{4,68},{68... | collective-permute-start | bytes 1769480 | tf_op jit(solution)/shard_map/ppermute | solution.py:75
  98.6 10.8 %copy-start.4 = (f32[1,768,192]{1,2,0:T(8,128)S(1)}, f32[1,768,192]{1,2,0:T(8,128)}, u32[]{:S(2)}) copy-start(f32[1,768,192]{1,2,0:T(8,128)} %param.17) | copy-start | bytes 1769476
  106.4 2.1 %collective-permute-start.26 = (f32[192,768]{1,0:T(8,128)S(1)}, f32[192,768]{1,0:T(8,128)S(1)}, u32[]{:S(2)}, u32[]{:S(2)}) collective-permute-start(f32[192,768]{1,0:T(8,128)S(1)} %collective-permute-done.18.refs_4_), channel_id=1, source_target_pairs={{0,64},{64,0},{1,65},{65,1},{2,66},{66,2},{3,67},{67,3},{4,68},{68... | collective-permute-start | bytes 1769480 | tf_op jit(solution)/shard_map/ppermute | solution.py:75
  106.9 2.5 %collective-permute-start.27 = (f32[192,768]{1,0:T(8,128)S(1)}, f32[192,768]{1,0:T(8,128)S(1)}, u32[]{:S(2)}, u32[]{:S(2)}) collective-permute-start(f32[192,768]{1,0:T(8,128)S(1)} %collective-permute-done.19.refs_5_), channel_id=1, source_target_pairs={{0,64},{64,0},{1,65},{65,1},{2,66},{66,2},{3,67},{67,3},{4,68},{68... | collective-permute-start | bytes 1769480 | tf_op jit(solution)/shard_map/ppermute | solution.py:75

commit v3 on v2

--- a/solution.py
+++ b/solution.py
@@ -210,65 +210,67 @@
     return tuple(pl.ds(pl.multiple_of(at * wide, 128), wide) for at in (core, 1 - core))
 
 
-def orthogonalized(full_ref):
-    iterate = normalized(full_ref[...])
-    for _ in range(NS_STEPS):
-        iterate = sweep(iterate)
-    full_ref[...] = iterate
-
-
-def finish_q_kernel(core_ref, *refs):
+def finish_kernel(core_ref, *refs):
     packs = [refs[i * LENT : (i + 1) * LENT] for i in range(4)]
-    peak_ref, peak_other_ref, mom_ref, mom_other_ref, weight_ref = refs[4 * LENT : -4]
-    out_mom_ref, out_upd_ref, out_weight_ref, full_ref = refs[-4:]
-    own, other = shares(core_ref, full_ref)
-    full_ref[:, own] = momentum_rate * mom_ref[...]
-    full_ref[:, other] = momentum_rate * mom_other_ref[...]
+    rest = refs[4 * LENT :]
+    one_kv_ref, two_kv_ref, peak_ref, peak_other_ref = rest[:4]
+    mom_q_ref, mom_q_other_ref, mom_kv_ref, mom_kv_other_ref = rest[4:8]
+    weight_q_ref, weight_kv_ref = rest[8:10]
+    out_mom_q_ref, out_upd_q_ref, out_weight_q_ref = rest[10:13]
+    out_mom_kv_ref, out_upd_kv_ref, out_weight_kv_ref, full_q_ref, full_kv_ref = rest[13:]
+    own_q, other_q = shares(core_ref, full_q_ref)
+    own_kv, other_kv = shares(core_ref, full_kv_ref)
+    full_q_ref[:, own_q] = momentum_rate * mom_q_ref[...]
+    full_q_ref[:, other_q] = momentum_rate * mom_q_other_ref[...]
     at = 0
     for one, one_swapped, two, two_swapped in zip(*packs):
         wide = one.shape[1]
-        full_ref[:, at : at + wide] += (one[...] + one_swapped[...]) + (
+        full_q_ref[:, at : at + wide] += (one[...] + one_swapped[...]) + (
             two[...] + two_swapped[...]
         )
         at += wide
-    out_mom_ref[...] = full_ref[:, own]
-    orthogonalized(full_ref)
-    update = (0.2 * math.sqrt(full_ref.shape[1])) * full_ref[:, own]
-    out_upd_ref[...] = update
+    full_kv_ref[:, own_kv] = momentum_rate * mom_kv_ref[...].T
+    full_kv_ref[:, other_kv] = momentum_rate * mom_kv_other_ref[...].T
+    full_kv_ref[...] += one_kv_ref[...] + two_kv_ref[...]
+    out_mom_q_ref[...] = full_q_ref[:, own_q]
+    out_mom_kv_ref[...] = full_kv_ref[:, own_kv].T
+    x_q = normalized(full_q_ref[...])
+    x_kv = normalized(full_kv_ref[...])
+    for _ in range(NS_STEPS):
+        x_q = sweep(x_q)
+        x_kv = sweep(x_kv)
+    full_q_ref[...] = x_q
+    full_kv_ref[...] = x_kv
     factor = clip_factor(peak_ref, peak_other_ref)
-    rows = lax.broadcasted_iota(jnp.int32, update.shape, 0)
-    scale = jnp.where(rows < QN, jnp.sqrt(factor), factor)
-    out_weight_ref[...] = (weight_ref[...] - learn_rate * update) * scale
-
-
-def finish_kv_kernel(core_ref, *refs):
-    one, one_swapped, peak_ref, peak_other_ref, mom_ref, mom_other_ref, weight_ref = refs[:7]
-    out_mom_ref, out_upd_ref, out_weight_ref, full_ref = refs[7:]
-    own, other = shares(core_ref, full_ref)
-    full_ref[:, own] = momentum_rate * mom_ref[...].T
-    full_ref[:, other] = momentum_rate * mom_other_ref[...].T
-    full_ref[...] += one[...] + one_swapped[...]
-    out_mom_ref[...] = full_ref[:, own].T
-    orthogonalized(full_ref)
-    update = ((0.2 * math.sqrt(full_ref.shape[1])) * full_ref[:, own]).T
-    out_upd_ref[...] = update
-    root = jnp.sqrt(clip_factor(peak_ref, peak_other_ref))
-    columns = lax.broadcasted_iota(jnp.int32, update.shape, 1)
-    scale = jnp.where(columns < KN, root, 1.0)
-    out_weight_ref[...] = (weight_ref[...] - learn_rate * update) * scale
-
-
-def finish(kernel, full_shape, core, *arrays):
-    shape = jax.ShapeDtypeStruct(arrays[-1].shape, F32)
+    root = jnp.sqrt(factor)
+    update_q = (0.2 * math.sqrt(full_q_ref.shape[1])) * full_q_ref[:, own_q]
+    out_upd_q_ref[...] = update_q
+    rows = lax.broadcasted_iota(jnp.int32, update_q.shape, 0)
+    scale_q = jnp.where(rows < QN, root, factor)
+    out_weight_q_ref[...] = (weight_q_ref[...] - learn_rate * update_q) * scale_q
+    update_kv = ((0.2 * math.sqrt(full_kv_ref.shape[1])) * full_kv_ref[:, own_kv]).T
+    out_upd_kv_ref[...] = update_kv
+    columns = lax.broadcasted_iota(jnp.int32, update_kv.shape, 1)
+    scale_kv = jnp.where(columns < KN, root, 1.0)
+    out_weight_kv_ref[...] = (weight_kv_ref[...] - learn_rate * update_kv) * scale_kv
+
+
+def finish(core, *arrays):
+    weight_q, weight_kv = arrays[-2:]
+    shape_q = jax.ShapeDtypeStruct(weight_q.shape, F32)
+    shape_kv = jax.ShapeDtypeStruct(weight_kv.shape, F32)
     return pl.pallas_call(
-        kernel,
-        out_shape=(shape,) * 3,
+        finish_kernel,
+        out_shape=(shape_q,) * 3 + (shape_kv,) * 3,
         in_specs=[SMEM] + [VMEM] * len(arrays),
-        out_specs=(VMEM,) * 3,
-        scratch_shapes=[pltpu.VMEM(full_shape, F32)],
+        out_specs=(VMEM,) * 6,
+        scratch_shapes=[
+            pltpu.VMEM((weight_q.shape[0], 2 * weight_q.shape[1]), F32),
+            pltpu.VMEM((weight_kv.shape[1], 2 * weight_kv.shape[0]), F32),
+        ],
         compiler_params=pltpu.CompilerParams(vmem_limit_bytes=20 * MIB),
         cost_estimate=pl.CostEstimate(
-            flops=10_000_000_000, bytes_accessed=8_000_000, transcendentals=0
+            flops=20_000_000_000, bytes_accessed=12_000_000, transcendentals=0
         ),
     )(core.reshape(1), *arrays)
 
@@ -286,9 +288,7 @@
 ):
     core = lax.axis_index("seq")
     device = core * CHIPS + lax.axis_index("fsdp")
-    width_q, rank_q = momentum_q.shape[2], latent_q.shape[1]
-    width_kv, rank_kv = momentum_kv.shape[2], latent_kv.shape[1]
-    unit = rank_q // LENT
+    unit = latent_q.shape[1] // LENT
     order = lax.dynamic_index_in_dim(jnp.asarray(block_orders()), device, keepdims=False)
     held = [latent_q[:, :unit], latent_q[:, unit:], latent_kv]
     grad_q = grad_q_heads.T
@@ -301,9 +301,9 @@
             got = lax.optimization_barrier(got)
             held = [jnp.concatenate([held[p], got[p]], axis=0) for p in range(PARTS)]
     partner = [exchange(send[p], p, 2, 0) for p in range(LENT)]
-    third = [exchange(held[p], p, 2, 1) for p in range(PARTS)]
+    third = [exchange(held[p], p, 2, 1) for p in range(LENT)]
+    third.append(exchange(after(held[2], partner[0]), 2, 2, 1))
     second = exchange(held[2], 2, 2, 0)
-    fourth = exchange(second, 2, 2, 1)
     order, row_peak, mom_q, mom_kv = after(
         (order, row_peak, momentum_q[0].T, momentum_kv[0]), held[0]
     )
@@ -311,6 +311,10 @@
     moms_q, moms_kv = (mom_q, swap(mom_q)), (mom_kv, swap(mom_kv))
     keep = arrange(0, order, grad_q)
     grad_kv = line_up(order, grad_kv_heads)
+    fourth = [
+        exchange(after(second, (keep, grad_kv))[: second.shape[0] // 2], 2, 2, 1),
+        exchange(after(third[2], partner)[third[2].shape[0] // 2 :], 2, 2, 0),
+    ]
     lent = multiply(0, held[:LENT], partner)
     own = multiply(0, held[:LENT], keep)
     own_kv = multiply(0, held[2:], [grad_kv])
@@ -319,22 +323,21 @@
     lent = multiply(1, third[:LENT], partner, lent)
     got = [exchange(lent[p], p, 2, 0) for p in range(LENT)]
     own = multiply(1, third[:LENT], keep, own)
-    (own_kv,) = multiply(3, [fourth], [grad_kv], own_kv)
-    new_mom_kv, upd_kv, new_weight_kv = finish(
-        finish_kv_kernel,
-        (width_kv, rank_kv),
+    own_kv = multiply(6, fourth[:1], [grad_kv], own_kv)
+    (own_kv,) = multiply(7, fourth[1:], [grad_kv], own_kv)
+    sums = (*own, *[swap(o) for o in own], *got, *[swap(g) for g in got])
+    outs = finish(
         core,
+        *sums,
         own_kv,
         swap(own_kv),
         *peaks,
+        *moms_q,
         *moms_kv,
+        weight_q[0].T,
         weight_kv[0],
     )
-    got = after(got, new_mom_kv)
-    sums = (*own, *[swap(o) for o in own], *got, *[swap(g) for g in got])
-    new_mom_q, upd_q, new_weight_q = finish(
-        finish_q_kernel, (width_q, rank_q), core, *sums, *peaks, *moms_q, weight_q[0].T
-    )
+    new_mom_q, upd_q, new_weight_q, new_mom_kv, upd_kv, new_weight_kv = outs
     return (
         new_mom_q.T[None],
         new_mom_kv[None],

time: 119 us -> 110 us (0.924)
  starting transfers between devices: 44.4 us -> 37.8 us
  Pallas kernels: 31.4 us -> 28.2 us
    ppermute x8, starting transfers between devices: 21.5 us -> 14 us  [swap(): return lax.ppermute(value, 'seq', [(0, 1), (1, 0)])]
    pallas_call x2 -> x1, Pallas kernels: 16.2 us -> 13 us  [finish(): pl.pallas_call(finish_kernel, out_shape=(shape_q,) * 3 + (shape_kv,) * 3,...]
    ppermute x21 -> x22, starting transfers between devices: 22.9 us -> 23.8 us  [exchange(): return lax.ppermute(value, ('seq', 'fsdp'), pairs)]
    ppermute x21 -> x22, waiting for transfers between devices: 35.3 us -> 35.6 us  [exchange(): return lax.ppermute(value, ('seq', 'fsdp'), pairs)]
    pallas_call x8 -> x9, Pallas kernels: 4.89 us -> 5.02 us  [multiply(): pl.pallas_call(functools.partial(multiply_kernel, slot, count), out_shape...]
  transfers between devices with their start and end apart: 29 -> 30, of which waited for: 14 -> 13; matrix products, arithmetic and copies ran while one was open for 1% -> 1% of each run, Pallas kernels for 19% -> 14%
where the time goes in v3:
time: 110 us; the launch traced here: 109 us
  waiting for transfers between devices  38.7 us (35%)
  starting transfers between devices  37.8 us (34%)
  Pallas kernels  28.2 us (26%)
  local copies, waits for them, and re-layouts  3.5 us (3%)
  between operations  1.1 us (1%)
    ppermute x22, waiting for transfers between devices, exchange(): return lax.ppermute(value, ('seq', 'fsdp'), pairs)  35.6 us
    ppermute x22, starting transfers between devices, exchange(): return lax.ppermute(value, ('seq', 'fsdp'), pairs)  23.8 us
    ppermute x8, starting transfers between devices, swap(): return lax.ppermute(value, 'seq', [(0, 1), (1, 0)])  14 us
    pallas_call x1, Pallas kernels, finish(): pl.pallas_call(finish_kernel, out_shape=(shape_q,) * 3 + (shape_kv,) * 3,...  13 us
    pallas_call x2, Pallas kernels, arrange(): pl.pallas_call(functools.partial(arrange_kernel, first), out_shape=(jax.S...  8.27 us
    pallas_call x9, Pallas kernels, multiply(): pl.pallas_call(functools.partial(multiply_kernel, slot, count), out_shape...  5.02 us
    ppermute x8, waiting for transfers between devices, swap(): return lax.ppermute(value, 'seq', [(0, 1), (1, 0)])  3.09 us
  transfers between devices with their start and end apart: 30, of which 13 were waited for; matrix products, arithmetic and copies ran while one was open for 1% of the time, Pallas kernels for 14%

profile of v3, /device:TPU:1, one launch (start us, length us, event | category | flops | bytes accessed | tf_op | source)
XLA Modules:
  0.0 109.5 jit_solution(12810105546776225514)
XLA Ops:
  0.6 1.0 fusion
  1.6 3.6 %collective-permute-start = (bf16[64,768]{1,0:T(8,128)(2,1)S(1)}, bf16[64,768]{1,0:T(8,128)(2,1)S(1)}, u32[]{:S(2)}, u32[]{:S(2)}) collective-permute-start(bf16[64,768]{1,0:T(8,128)(2,1)S(1)} %get-tuple-element.87), channel_id=1, source_target_pairs={{0,1},{1,0},{2,3},{3,2},{4,5},{5,4},{6,7},{7,6},{8,9},{9,8},{10,11... | collective-permute-start | bytes 294920 | tf_op jit(solution)/shard_map/ppermute | solution.py:90
  5.3 3.8 %collective-permute-start.1 = (bf16[64,768]{1,0:T(8,128)(2,1)S(1)}, bf16[64,768]{1,0:T(8,128)(2,1)S(1)}, u32[]{:S(2)}, u32[]{:S(2)}) collective-permute-start(bf16[64,768]{1,0:T(8,128)(2,1)S(1)} %get-tuple-element.86), channel_id=1, source_target_pairs={{0,4},{1,5},{2,6},{3,7},{4,0},{5,1},{6,2},{7,3},{8,12},{9,13},{10,... | collective-permute-start | bytes 294920 | tf_op jit(solution)/shard_map/ppermute | solution.py:90
  9.0 2.5 %collective-permute-start.2 = (bf16[64,512]{1,0:T(8,128)(2,1)}, bf16[64,512]{1,0:T(8,128)(2,1)S(1)}, u32[]{:S(2)}, u32[]{:S(2)}) collective-permute-start(bf16[64,512]{1,0:T(8,128)(2,1)} %param.11), channel_id=1, source_target_pairs={{0,16},{1,17},{2,18},{3,19},{4,20},{5,21},{6,22},{7,23},{8,24},{9,... | collective-permute-start | bytes 196616 | tf_op jit(solution)/shard_map/ppermute | solution.py:90
  11.5 0.7 constant_dynamic-slice_fusion
  12.2 1.4 %copy-done = bf16[4096,192]{0,1:T(8,128)(2,1)S(1)} copy-done((bf16[4096,192]{0,1:T(8,128)(2,1)S(1)}, bf16[4096,192]{0,1:T(8,128)(2,1)}, u32[]{:S(2)}) %copy-start) | copy-done | bytes 1572888
  13.6 4.1 %shard_map.145 = (bf16[192,2048]{1,0:T(8,128)(2,1)S(1)}, bf16[192,2048]{1,0:T(8,128)(2,1)S(1)}) custom-call(s32[192]{0:T(256)S(1)} %bitcast.25, bf16[192,4096]{1,0:T(8,128)(2,1)S(1)} %bitcast.23), custom_call_target="tpu_custom_call" | custom-call | bytes 10000000 | tf_op jit(solution)/shard_map/pallas_call | solution.py:136
  17.9 0.1 collective-permute-start.3
  18.0 0.1 collective-permute-start.4
  18.0 0.1 collective-permute-start.5
  18.1 4.1 %collective-permute-done.5 = bf16[128,512]{1,0:T(8,128)(2,1)S(1)} collective-permute-done((bf16[128,512]{1,0:T(8,128)(2,1)S(1)}, bf16[128,512]{1,0:T(8,128)(2,1)S(1)}, u32[]{:S(2)}, u32[]{:S(2)}) %collective-permute-start.5) | collective-permute-done | bytes 131104 | tf_op jit(solution)/shard_map/ppermute | solution.py:90
  22.2 0.5 collective-permute-done.3
  22.8 0.1 collective-permute-done.4
  22.9 0.3 collective-permute-start.7
  23.2 0.1 collective-permute-start.6
  23.3 0.6 collective-permute-start.8
  23.9 5.9 %collective-permute-done.8 = bf16[256,512]{1,0:T(8,128)(2,1)S(1)} collective-permute-done((bf16[256,512]{1,0:T(8,128)(2,1)S(1)}, bf16[256,512]{1,0:T(8,128)(2,1)S(1)}, u32[]{:S(2)}, u32[]{:S(2)}) %collective-permute-start.8) | collective-permute-done | bytes 262176 | tf_op jit(solution)/shard_map/ppermute | solution.py:90
  29.8 1.0 collective-permute-done.7
  30.8 0.3 collective-permute-done.6
  31.1 0.1 pad_maximum_fusion.1
  31.2 0.1 collective-permute-start.10
  31.3 0.1 pad_maximum_fusion
  31.3 0.5 collective-permute-start.9
  31.9 1.5 %collective-permute-start.11 = (bf16[512,512]{1,0:T(8,128)(2,1)S(1)}, bf16[512,512]{1,0:T(8,128)(2,1)S(1)}, u32[]{:S(2)}, u32[]{:S(2)}) collective-permute-start(bf16[512,512]{1,0:T(8,128)(2,1)S(1)} %pad_maximum_fusion.2), channel_id=1, source_target_pairs={{0,3},{1,2},{2,1},{3,0},{4,7},{5,6},{6,5},{7,4},{8,11},{9,10},{10,... | collective-permute-start | bytes 1572872 | tf_op jit(solution)/shard_map/ppermute | solution.py:90
  33.5 6.8 %collective-permute-done.11 = bf16[512,512]{1,0:T(8,128)(2,1)S(1)} collective-permute-done((bf16[512,512]{1,0:T(8,128)(2,1)S(1)}, bf16[512,512]{1,0:T(8,128)(2,1)S(1)}, u32[]{:S(2)}, u32[]{:S(2)}) %collective-permute-start.11) | collective-permute-done | bytes 524320 | tf_op jit(solution)/shard_map/ppermute | solution.py:90
  40.3 2.0 %collective-permute-done.10 = bf16[512,768]{1,0:T(8,128)(2,1)S(1)} collective-permute-done((bf16[512,768]{1,0:T(8,128)(2,1)S(1)}, bf16[512,768]{1,0:T(8,128)(2,1)S(1)}, u32[]{:S(2)}, u32[]{:S(2)}) %collective-permute-start.10) | collective-permute-done | bytes 786464 | tf_op jit(solution)/shard_map/ppermute | solution.py:90
  42.4 0.2 collective-permute-done.9
  42.5 0.1 constant_dynamic-update-slice_fusion.4.refs_1_
  42.6 1.4 %collective-permute-start.13 = (bf16[1024,768]{1,0:T(8,128)(2,1)S(1)}, bf16[1024,768]{1,0:T(8,128)(2,1)S(1)}, u32[]{:S(2)}, u32[]{:S(2)}) collective-permute-start(bf16[1024,768]{1,0:T(8,128)(2,1)S(1)} %constant_dynamic-update-slice_fusion.4.refs_1_), channel_id=1, source_target_pairs={{0,3},{1,2},{2,1},{3,0},{4,7},{5,6},{6,5},{7,4},{8,11},{9,10},{10,... | collective-permute-start | bytes 4718600 | tf_op jit(solution)/shard_map/ppermute | solution.py:90
  44.0 0.1 constant_dynamic-update-slice_fusion.refs_0_
  44.1 1.4 %collective-permute-start.12 = (bf16[1024,768]{1,0:T(8,128)(2,1)S(1)}, bf16[1024,768]{1,0:T(8,128)(2,1)S(1)}, u32[]{:S(2)}, u32[]{:S(2)}) collective-permute-start(bf16[1024,768]{1,0:T(8,128)(2,1)S(1)} %constant_dynamic-update-slice_fusion.refs_0_), channel_id=1, source_target_pairs={{0,48},{1,49},{2,50},{3,51},{4,52},{5,53},{6,54},{7,55},{8,56},{9,... | collective-permute-start | bytes 4718600 | tf_op jit(solution)/shard_map/ppermute | solution.py:90
  45.5 2.7 %collective-permute-start.16 = (bf16[192,2048]{1,0:T(8,128)(2,1)S(1)}, bf16[192,2048]{1,0:T(8,128)(2,1)S(1)}, u32[]{:S(2)}, u32[]{:S(2)}) collective-permute-start(bf16[192,2048]{1,0:T(8,128)(2,1)S(1)} %get-tuple-element.49), channel_id=1, source_target_pairs={{0,16},{1,17},{2,18},{3,19},{4,20},{5,21},{6,22},{7,23},{8,24},{9,... | collective-permute-start | bytes 2359304 | tf_op jit(solution)/shard_map/ppermute | solution.py:90
  48.1 0.0 copy-start.2
  48.2 0.5 collective-permute-start.24
  48.8 0.6 collective-permute-start.17
  49.4 13.2 %collective-permute-done.16.refs_2_ = bf16[192,2048]{1,0:T(8,128)(2,1)S(1)} collective-permute-done((bf16[192,2048]{1,0:T(8,128)(2,1)S(1)}, bf16[192,2048]{1,0:T(8,128)(2,1)S(1)}, u32[]{:S(2)}, u32[]{:S(2)}) %collective-permute-start.16) | collective-permute-done | bytes 786464 | tf_op jit(solution)/shard_map/ppermute | solution.py:90
  62.6 4.1 %shard_map.146 = (bf16[192,2048]{1,0:T(8,128)(2,1)S(1)}, bf16[192,2048]{1,0:T(8,128)(2,1)S(1)}) custom-call(s32[192]{0:T(256)S(1)} %bitcast.26, bf16[192,4096]{1,0:T(8,128)(2,1)S(1)} %bitcast.24), custom_call_target="tpu_custom_call" | custom-call | bytes 10000000 | tf_op jit(solution)/shard_map/pallas_call | solution.py:136
  66.7 2.0 %shard_map.151.refs_1_ = bf16[256,4096]{1,0:T(8,128)(2,1)S(1)} custom-call(s32[192]{0:T(256)S(1)} %bitcast.27, bf16[4096,256]{1,0:T(8,128)(2,1)S(1)} %copy-done.2), custom_call_target="tpu_custom_call" | custom-call | bytes 10000000 | tf_op jit(solution)/shard_map/pallas_call | solution.py:162
  68.7 0.4 shard_map.152.refs_2_
  69.1 0.0 copy-start.7
  69.1 0.8 shard_map.147
  70.0 2.8 %collective-permute-start.27 = (f32[1,4096]{1,0:T(1,128)S(1)}, f32[1,4096]{1,0:T(1,128)S(1)}, u32[]{:S(2)}, u32[]{:S(2)}) collective-permute-start(f32[1,4096]{1,0:T(1,128)S(1)} %copy-done.7), channel_id=1, source_target_pairs={{0,64},{64,0},{1,65},{65,1},{2,66},{66,2},{3,67},{67,3},{4,68},{68... | collective-permute-start | bytes 49160 | tf_op jit(solution)/shard_map/ppermute | solution.py:75
  72.7 0.8 shard_map.149
  73.6 0.4 collective-permute-start.25
  74.0 0.8 shard_map.150
  74.8 2.1 %collective-permute-start.18 = (f32[192,768]{1,0:T(8,128)S(1)}, f32[192,768]{1,0:T(8,128)S(1)}, u32[]{:S(2)}, u32[]{:S(2)}) collective-permute-start(f32[192,768]{1,0:T(8,128)S(1)} %get-tuple-element.71), channel_id=1, source_target_pairs={{0,16},{1,17},{2,18},{3,19},{4,20},{5,21},{6,22},{7,23},{8,24},{9,... | collective-permute-start | bytes 1769480 | tf_op jit(solution)/shard_map/ppermute | solution.py:90
  76.9 0.9 collective-permute-start.19
  77.8 0.4 shard_map.153.refs_2_
  78.3 4.4 %collective-permute-start.28 = (f32[192,768]{1,0:T(8,128)S(1)}, f32[192,768]{1,0:T(8,128)S(1)}, u32[]{:S(2)}, u32[]{:S(2)}) collective-permute-start(f32[192,768]{1,0:T(8,128)S(1)} %bitcast.28), channel_id=1, source_target_pairs={{0,64},{64,0},{1,65},{65,1},{2,66},{66,2},{3,67},{67,3},{4,68},{68... | collective-permute-start | bytes 1769480 | tf_op jit(solution)/shard_map/ppermute | solution.py:75
  82.7 0.0 copy-start.5
  82.7 0.5 collective-permute-start.23
  83.3 0.4 shard_map.154.refs_2_
  83.7 5.3 %collective-permute-start.29 = (f32[256,256]{1,0:T(8,128)S(1)}, f32[256,256]{1,0:T(8,128)S(1)}, u32[]{:S(2)}, u32[]{:S(2)}) collective-permute-start(f32[256,256]{1,0:T(8,128)S(1)} %bitcast.31), channel_id=1, source_target_pairs={{0,64},{64,0},{1,65},{65,1},{2,66},{66,2},{3,67},{67,3},{4,68},{68... | collective-permute-start | bytes 786440 | tf_op jit(solution)/shard_map/ppermute | solution.py:75
  89.0 0.3 shard_map.155.refs_2_
  89.3 0.8 shard_map.148
  90.1 0.1 collective-permute-done.29.refs_15_
  90.2 0.4 collective-permute-start.14
  90.6 1.5 %collective-permute-done.23.refs_0_ = bf16[512,512]{1,0:T(8,128)(2,1)S(1)} collective-permute-done((bf16[512,512]{1,0:T(8,128)(2,1)S(1)}, bf16[512,512]{1,0:T(8,128)(2,1)S(1)}, u32[]{:S(2)}, u32[]{:S(2)}) %collective-permute-start.23) | collective-permute-done | bytes 524320 | tf_op jit(solution)/shard_map/ppermute | solution.py:90
  92.1 0.5 collective-permute-start.20
  92.6 0.1 collective-permute-start.21
  92.7 0.3 shard_map.156.refs_8_
  93.0 0.5 collective-permute-start.26
  93.5 3.0 %collective-permute-done.26.refs_9_ = f32[256,512]{1,0:T(8,128)S(1)} collective-permute-done((f32[256,512]{1,0:T(8,128)S(1)}, f32[256,512]{1,0:T(8,128)S(1)}, u32[]{:S(2)}, u32[]{:S(2)}) %collective-permute-start.26) | collective-permute-done | bytes 524320 | tf_op jit(solution)/shard_map/ppermute | solution.py:75
  96.5 13.0 %shard_map.157 = (f32[192,768]{1,0:T(8,128)}, f32[192,768]{1,0:T(8,128)}, f32[192,768]{1,0:T(8,128)}, f32[256,256]{1,0:T(8,128)}, f32[256,256]{1,0:T(8,128)}, /*index=5*/f32[256,256]{1,0:T(8,128)}) custom-call(s32[1]{0:T(128)} %bitcast.core_ref, f32[192,768]{1,0:T(8,128)S(1)} %get-tuple-element.66.refs_0_, f32[192,768]{1,0:T(8,128)S(1)} %get-tuple-element.67.refs_1_, ...), custom_call_target="tpu_custom_call" | custom-call | flops 20000000000 | bytes 12000000 | tf_op jit(solution)/shard_map/pallas_call | solution.py:262
  (51 shorter events, 0.5 us)
Async XLA Ops:
  0.6 17.2 %copy-start.8 = (bf16[64,512]{1,0:T(8,128)(2,1)S(1)}, bf16[64,512]{1,0:T(8,128)(2,1)}, u32[]{:S(2)}) copy-start(bf16[64,512]{1,0:T(8,128)(2,1)} %param.11) | copy-start | bytes 196612
  1.6 16.1 %collective-permute-start = (bf16[64,768]{1,0:T(8,128)(2,1)S(1)}, bf16[64,768]{1,0:T(8,128)(2,1)S(1)}, u32[]{:S(2)}, u32[]{:S(2)}) collective-permute-start(bf16[64,768]{1,0:T(8,128)(2,1)S(1)} %get-tuple-element.87), channel_id=1, source_target_pairs={{0,1},{1,0},{2,3},{3,2},{4,5},{5,4},{6,7},{7,6},{8,9},{9,8},{10,11... | collective-permute-start | bytes 294920 | tf_op jit(solution)/shard_map/ppermute | solution.py:90
  5.3 12.5 %collective-permute-start.1 = (bf16[64,768]{1,0:T(8,128)(2,1)S(1)}, bf16[64,768]{1,0:T(8,128)(2,1)S(1)}, u32[]{:S(2)}, u32[]{:S(2)}) collective-permute-start(bf16[64,768]{1,0:T(8,128)(2,1)S(1)} %get-tuple-element.86), channel_id=1, source_target_pairs={{0,4},{1,5},{2,6},{3,7},{4,0},{5,1},{6,2},{7,3},{8,12},{9,13},{10,... | collective-permute-start | bytes 294920 | tf_op jit(solution)/shard_map/ppermute | solution.py:90
  9.0 8.7 %collective-permute-start.2 = (bf16[64,512]{1,0:T(8,128)(2,1)}, bf16[64,512]{1,0:T(8,128)(2,1)S(1)}, u32[]{:S(2)}, u32[]{:S(2)}) collective-permute-start(bf16[64,512]{1,0:T(8,128)(2,1)} %param.11), channel_id=1, source_target_pairs={{0,16},{1,17},{2,18},{3,19},{4,20},{5,21},{6,22},{7,23},{8,24},{9,... | collective-permute-start | bytes 196616 | tf_op jit(solution)/shard_map/ppermute | solution.py:90
  12.2 1.4 %copy-start = (bf16[4096,192]{0,1:T(8,128)(2,1)S(1)}, bf16[4096,192]{0,1:T(8,128)(2,1)}, u32[]{:S(2)}) copy-start(bf16[4096,192]{0,1:T(8,128)(2,1)} %param.12) | copy-start | bytes 4718596
  17.9 4.9 %collective-permute-start.3 = (bf16[128,768]{1,0:T(8,128)(2,1)S(1)}, bf16[128,768]{1,0:T(8,128)(2,1)S(1)}, u32[]{:S(2)}, u32[]{:S(2)}) collective-permute-start(bf16[128,768]{1,0:T(8,128)(2,1)S(1)} %get-tuple-element.50), channel_id=1, source_target_pairs={{0,3},{1,2},{2,1},{3,0},{4,7},{5,6},{6,5},{7,4},{8,11},{9,10},{10,... | collective-permute-start | bytes 589832 | tf_op jit(solution)/shard_map/ppermute | solution.py:90
  18.0 4.9 %collective-permute-start.4 = (bf16[128,768]{1,0:T(8,128)(2,1)S(1)}, bf16[128,768]{1,0:T(8,128)(2,1)S(1)}, u32[]{:S(2)}, u32[]{:S(2)}) collective-permute-start(bf16[128,768]{1,0:T(8,128)(2,1)S(1)} %get-tuple-element.51), channel_id=1, source_target_pairs={{0,12},{1,13},{2,14},{3,15},{4,8},{5,9},{6,10},{7,11},{8,4},{9,5},... | collective-permute-start | bytes 589832 | tf_op jit(solution)/shard_map/ppermute | solution.py:90
  18.0 4.2 %collective-permute-start.5 = (bf16[128,512]{1,0:T(8,128)(2,1)S(1)}, bf16[128,512]{1,0:T(8,128)(2,1)S(1)}, u32[]{:S(2)}, u32[]{:S(2)}) collective-permute-start(bf16[128,512]{1,0:T(8,128)(2,1)S(1)} %pad_maximum_fusion.8), channel_id=1, source_target_pairs={{0,48},{1,49},{2,50},{3,51},{4,52},{5,53},{6,54},{7,55},{8,56},{9,... | collective-permute-start | bytes 393224 | tf_op jit(solution)/shard_map/ppermute | solution.py:90
  22.9 7.9 %collective-permute-start.7 = (bf16[256,768]{1,0:T(8,128)(2,1)S(1)}, bf16[256,768]{1,0:T(8,128)(2,1)S(1)}, u32[]{:S(2)}, u32[]{:S(2)}) collective-permute-start(bf16[256,768]{1,0:T(8,128)(2,1)S(1)} %pad_maximum_fusion.4), channel_id=1, source_target_pairs={{0,16},{1,17},{2,18},{3,19},{4,20},{5,21},{6,22},{7,23},{8,24},{9,... | collective-permute-start | bytes 1179656 | tf_op jit(solution)/shard_map/ppermute | solution.py:90
  23.2 7.9 %collective-permute-start.6 = (bf16[256,768]{1,0:T(8,128)(2,1)S(1)}, bf16[256,768]{1,0:T(8,128)(2,1)S(1)}, u32[]{:S(2)}, u32[]{:S(2)}) collective-permute-start(bf16[256,768]{1,0:T(8,128)(2,1)S(1)} %pad_maximum_fusion.3), channel_id=1, source_target_pairs={{0,4},{1,5},{2,6},{3,7},{4,0},{5,1},{6,2},{7,3},{8,12},{9,13},{10,... | collective-permute-start | bytes 1179656 | tf_op jit(solution)/shard_map/ppermute | solution.py:90
  23.3 6.5 %collective-permute-start.8 = (bf16[256,512]{1,0:T(8,128)(2,1)S(1)}, bf16[256,512]{1,0:T(8,128)(2,1)S(1)}, u32[]{:S(2)}, u32[]{:S(2)}) collective-permute-start(bf16[256,512]{1,0:T(8,128)(2,1)S(1)} %pad_maximum_fusion.5), channel_id=1, source_target_pairs={{0,1},{1,0},{2,3},{3,2},{4,5},{5,4},{6,7},{7,6},{8,9},{9,8},{10,11... | collective-permute-start | bytes 786440 | tf_op jit(solution)/shard_map/ppermute | solution.py:90
  31.2 11.2 %collective-permute-start.10 = (bf16[512,768]{1,0:T(8,128)(2,1)S(1)}, bf16[512,768]{1,0:T(8,128)(2,1)S(1)}, u32[]{:S(2)}, u32[]{:S(2)}) collective-permute-start(bf16[512,768]{1,0:T(8,128)(2,1)S(1)} %pad_maximum_fusion.1), channel_id=1, source_target_pairs={{0,48},{1,49},{2,50},{3,51},{4,52},{5,53},{6,54},{7,55},{8,56},{9,... | collective-permute-start | bytes 2359304 | tf_op jit(solution)/shard_map/ppermute | solution.py:90
  31.3 11.2 %collective-permute-start.9 = (bf16[512,768]{1,0:T(8,128)(2,1)S(1)}, bf16[512,768]{1,0:T(8,128)(2,1)S(1)}, u32[]{:S(2)}, u32[]{:S(2)}) collective-permute-start(bf16[512,768]{1,0:T(8,128)(2,1)S(1)} %pad_maximum_fusion), channel_id=1, source_target_pairs={{0,12},{1,13},{2,14},{3,15},{4,8},{5,9},{6,10},{7,11},{8,4},{9,5},... | collective-permute-start | bytes 2359304 | tf_op jit(solution)/shard_map/ppermute | solution.py:90
  31.9 8.4 %collective-permute-start.11 = (bf16[512,512]{1,0:T(8,128)(2,1)S(1)}, bf16[512,512]{1,0:T(8,128)(2,1)S(1)}, u32[]{:S(2)}, u32[]{:S(2)}) collective-permute-start(bf16[512,512]{1,0:T(8,128)(2,1)S(1)} %pad_maximum_fusion.2), channel_id=1, source_target_pairs={{0,3},{1,2},{2,1},{3,0},{4,7},{5,6},{6,5},{7,4},{8,11},{9,10},{10,... | collective-permute-start | bytes 1572872 | tf_op jit(solution)/shard_map/ppermute | solution.py:90
  42.6 20.0 %copy-start.1 = (bf16[4096,192]{0,1:T(8,128)(2,1)S(1)}, bf16[4096,192]{0,1:T(8,128)(2,1)}, u32[]{:S(2)}) copy-start(bf16[4096,192]{0,1:T(8,128)(2,1)} %param.12) | copy-start | bytes 4718596
  42.6 31.4 %collective-permute-start.13 = (bf16[1024,768]{1,0:T(8,128)(2,1)S(1)}, bf16[1024,768]{1,0:T(8,128)(2,1)S(1)}, u32[]{:S(2)}, u32[]{:S(2)}) collective-permute-start(bf16[1024,768]{1,0:T(8,128)(2,1)S(1)} %constant_dynamic-update-slice_fusion.4.refs_1_), channel_id=1, source_target_pairs={{0,3},{1,2},{2,1},{3,0},{4,7},{5,6},{6,5},{7,4},{8,11},{9,10},{10,... | collective-permute-start | bytes 4718600 | tf_op jit(solution)/shard_map/ppermute | solution.py:90
  44.1 29.9 %collective-permute-start.12 = (bf16[1024,768]{1,0:T(8,128)(2,1)S(1)}, bf16[1024,768]{1,0:T(8,128)(2,1)S(1)}, u32[]{:S(2)}, u32[]{:S(2)}) collective-permute-start(bf16[1024,768]{1,0:T(8,128)(2,1)S(1)} %constant_dynamic-update-slice_fusion.refs_0_), channel_id=1, source_target_pairs={{0,48},{1,49},{2,50},{3,51},{4,52},{5,53},{6,54},{7,55},{8,56},{9,... | collective-permute-start | bytes 4718600 | tf_op jit(solution)/shard_map/ppermute | solution.py:90
  45.5 17.1 %collective-permute-start.16 = (bf16[192,2048]{1,0:T(8,128)(2,1)S(1)}, bf16[192,2048]{1,0:T(8,128)(2,1)S(1)}, u32[]{:S(2)}, u32[]{:S(2)}) collective-permute-start(bf16[192,2048]{1,0:T(8,128)(2,1)S(1)} %get-tuple-element.49), channel_id=1, source_target_pairs={{0,16},{1,17},{2,18},{3,19},{4,20},{5,21},{6,22},{7,23},{8,24},{9,... | collective-permute-start | bytes 2359304 | tf_op jit(solution)/shard_map/ppermute | solution.py:90
  48.1 18.6 %copy-start.2 = (bf16[4096,256]{1,0:T(8,128)(2,1)S(1)}, bf16[4096,256]{1,0:T(8,128)(2,1)}, u32[]{:S(2)}) copy-start(bf16[4096,256]{1,0:T(8,128)(2,1)} %grad_ref.1) | copy-start | bytes 6291460
  48.2 25.3 %collective-permute-start.24 = (bf16[1024,512]{1,0:T(8,128)(2,1)S(1)}, bf16[1024,512]{1,0:T(8,128)(2,1)S(1)}, u32[]{:S(2)}, u32[]{:S(2)}) collective-permute-start(bf16[1024,512]{1,0:T(8,128)(2,1)S(1)} %constant_dynamic-update-slice_fusion.8.refs_0_), channel_id=1, source_target_pairs={{0,4},{1,5},{2,6},{3,7},{4,0},{5,1},{6,2},{7,3},{8,12},{9,13},{10,... | collective-permute-start | bytes 3145736 | tf_op jit(solution)/shard_map/ppermute | solution.py:90
  48.8 21.2 %collective-permute-start.17 = (bf16[192,2048]{1,0:T(8,128)(2,1)S(1)}, bf16[192,2048]{1,0:T(8,128)(2,1)S(1)}, u32[]{:S(2)}, u32[]{:S(2)}) collective-permute-start(bf16[192,2048]{1,0:T(8,128)(2,1)S(1)} %get-tuple-element.68), channel_id=1, source_target_pairs={{0,1},{1,0},{2,3},{3,2},{4,5},{5,4},{6,7},{7,6},{8,9},{9,8},{10,11... | collective-permute-start | bytes 2359304 | tf_op jit(solution)/shard_map/ppermute | solution.py:90
  62.5 15.7 %collective-permute-start.22 = (bf16[1024,512]{1,0:T(8,128)(2,1)S(1)}, bf16[1024,512]{1,0:T(8,128)(2,1)S(1)}, u32[]{:S(2)}, u32[]{:S(2)}) collective-permute-start(bf16[1024,512]{1,0:T(8,128)(2,1)S(1)} %constant_dynamic-update-slice_fusion.8.refs_0_), channel_id=1, source_target_pairs={{0,12},{1,13},{2,14},{3,15},{4,8},{5,9},{6,10},{7,11},{8,4},{9,5},... | collective-permute-start | bytes 3145736 | tf_op jit(solution)/shard_map/ppermute | solution.py:90
  69.1 0.8 copy-start.7
  70.0 12.8 %collective-permute-start.27 = (f32[1,4096]{1,0:T(1,128)S(1)}, f32[1,4096]{1,0:T(1,128)S(1)}, u32[]{:S(2)}, u32[]{:S(2)}) collective-permute-start(f32[1,4096]{1,0:T(1,128)S(1)} %copy-done.7), channel_id=1, source_target_pairs={{0,64},{64,0},{1,65},{65,1},{2,66},{66,2},{3,67},{67,3},{4,68},{68... | collective-permute-start | bytes 49160 | tf_op jit(solution)/shard_map/ppermute | solution.py:75
  73.6 10.1 %collective-permute-start.25 = (bf16[512,512]{1,0:T(8,128)(2,1)S(1)}, bf16[512,512]{1,0:T(8,128)(2,1)S(1)}, u32[]{:S(2)}, u32[]{:S(2)}) collective-permute-start(bf16[512,512]{1,0:T(8,128)(2,1)S(1)} %slice.15), channel_id=1, source_target_pairs={{0,12},{1,13},{2,14},{3,15},{4,8},{5,9},{6,10},{7,11},{8,4},{9,5},... | collective-permute-start | bytes 1572872 | tf_op jit(solution)/shard_map/ppermute | solution.py:90
  74.8 17.3 %collective-permute-start.18 = (f32[192,768]{1,0:T(8,128)S(1)}, f32[192,768]{1,0:T(8,128)S(1)}, u32[]{:S(2)}, u32[]{:S(2)}) collective-permute-start(f32[192,768]{1,0:T(8,128)S(1)} %get-tuple-element.71), channel_id=1, source_target_pairs={{0,16},{1,17},{2,18},{3,19},{4,20},{5,21},{6,22},{7,23},{8,24},{9,... | collective-permute-start | bytes 1769480 | tf_op jit(solution)/shard_map/ppermute | solution.py:90
  76.9 1.4 %copy-start.3 = (f32[1,768,192]{1,2,0:T(8,128)S(1)}, f32[1,768,192]{1,2,0:T(8,128)}, u32[]{:S(2)}) copy-start(f32[1,768,192]{1,2,0:T(8,128)} %param.15) | copy-start | bytes 1769476
  76.9 15.7 %collective-permute-start.19 = (f32[192,768]{1,0:T(8,128)S(1)}, f32[192,768]{1,0:T(8,128)S(1)}, u32[]{:S(2)}, u32[]{:S(2)}) collective-permute-start(f32[192,768]{1,0:T(8,128)S(1)} %get-tuple-element.72), channel_id=1, source_target_pairs={{0,1},{1,0},{2,3},{3,2},{4,5},{5,4},{6,7},{7,6},{8,9},{9,8},{10,11... | collective-permute-start | bytes 1769480 | tf_op jit(solution)/shard_map/ppermute | solution.py:90
  78.3 14.7 %collective-permute-start.28 = (f32[192,768]{1,0:T(8,128)S(1)}, f32[192,768]{1,0:T(8,128)S(1)}, u32[]{:S(2)}, u32[]{:S(2)}) collective-permute-start(f32[192,768]{1,0:T(8,128)S(1)} %bitcast.28), channel_id=1, source_target_pairs={{0,64},{64,0},{1,65},{65,1},{2,66},{66,2},{3,67},{67,3},{4,68},{68... | collective-permute-start | bytes 1769480 | tf_op jit(solution)/shard_map/ppermute | solution.py:75
  82.7 1.0 copy-start.5
  82.7 9.3 %collective-permute-start.23 = (bf16[512,512]{1,0:T(8,128)(2,1)S(1)}, bf16[512,512]{1,0:T(8,128)(2,1)S(1)}, u32[]{:S(2)}, u32[]{:S(2)}) collective-permute-start(bf16[512,512]{1,0:T(8,128)(2,1)S(1)} %slice.14), channel_id=1, source_target_pairs={{0,4},{1,5},{2,6},{3,7},{4,0},{5,1},{6,2},{7,3},{8,12},{9,13},{10,... | collective-permute-start | bytes 1572872 | tf_op jit(solution)/shard_map/ppermute | solution.py:90
  83.7 6.5 %collective-permute-start.29 = (f32[256,256]{1,0:T(8,128)S(1)}, f32[256,256]{1,0:T(8,128)S(1)}, u32[]{:S(2)}, u32[]{:S(2)}) collective-permute-start(f32[256,256]{1,0:T(8,128)S(1)} %bitcast.31), channel_id=1, source_target_pairs={{0,64},{64,0},{1,65},{65,1},{2,66},{66,2},{3,67},{67,3},{4,68},{68... | collective-permute-start | bytes 786440 | tf_op jit(solution)/shard_map/ppermute | solution.py:75
  90.2 6.3 %collective-permute-start.14 = (f32[192,768]{1,0:T(8,128)S(1)}, f32[192,768]{1,0:T(8,128)S(1)}, u32[]{:S(2)}, u32[]{:S(2)}) collective-permute-start(f32[192,768]{1,0:T(8,128)S(1)} %get-tuple-element.66.refs_0_), channel_id=1, source_target_pairs={{0,64},{64,0},{1,65},{65,1},{2,66},{66,2},{3,67},{67,3},{4,68},{68... | collective-permute-start | bytes 1769480 | tf_op jit(solution)/shard_map/ppermute | solution.py:75
  92.0 4.5 %copy-start.4 = (f32[1,768,192]{1,2,0:T(8,128)S(1)}, f32[1,768,192]{1,2,0:T(8,128)}, u32[]{:S(2)}) copy-start(f32[1,768,192]{1,2,0:T(8,128)} %param.17) | copy-start | bytes 1769476
  92.0 4.5 %copy-start.6 = (f32[1,256,256]{2,1,0:T(8,128)S(1)}, f32[1,256,256]{2,1,0:T(8,128)}, u32[]{:S(2)}) copy-start(f32[1,256,256]{2,1,0:T(8,128)} %param.18) | copy-start | bytes 786436
  92.0 4.4 %collective-permute-start.15 = (f32[192,768]{1,0:T(8,128)S(1)}, f32[192,768]{1,0:T(8,128)S(1)}, u32[]{:S(2)}, u32[]{:S(2)}) collective-permute-start(f32[192,768]{1,0:T(8,128)S(1)} %get-tuple-element.67.refs_1_), channel_id=1, source_target_pairs={{0,64},{64,0},{1,65},{65,1},{2,66},{66,2},{3,67},{67,3},{4,68},{68... | collective-permute-start | bytes 1769480 | tf_op jit(solution)/shard_map/ppermute | solution.py:75
  92.1 4.4 %collective-permute-start.20 = (f32[192,768]{1,0:T(8,128)S(1)}, f32[192,768]{1,0:T(8,128)S(1)}, u32[]{:S(2)}, u32[]{:S(2)}) collective-permute-start(f32[192,768]{1,0:T(8,128)S(1)} %collective-permute-done.18.refs_4_), channel_id=1, source_target_pairs={{0,64},{64,0},{1,65},{65,1},{2,66},{66,2},{3,67},{67,3},{4,68},{68... | collective-permute-start | bytes 1769480 | tf_op jit(solution)/shard_map/ppermute | solution.py:75
  92.6 3.9 %collective-permute-start.21 = (f32[192,768]{1,0:T(8,128)S(1)}, f32[192,768]{1,0:T(8,128)S(1)}, u32[]{:S(2)}, u32[]{:S(2)}) collective-permute-start(f32[192,768]{1,0:T(8,128)S(1)} %collective-permute-done.19.refs_5_), channel_id=1, source_target_pairs={{0,64},{64,0},{1,65},{65,1},{2,66},{66,2},{3,67},{67,3},{4,68},{68... | collective-permute-start | bytes 1769480 | tf_op jit(solution)/shard_map/ppermute | solution.py:75
  93.0 3.5 %collective-permute-start.26 = (f32[256,512]{1,0:T(8,128)S(1)}, f32[256,512]{1,0:T(8,128)S(1)}, u32[]{:S(2)}, u32[]{:S(2)}) collective-permute-start(f32[256,512]{1,0:T(8,128)S(1)} %shard_map.156.refs_8_), channel_id=1, source_target_pairs={{0,64},{64,0},{1,65},{65,1},{2,66},{66,2},{3,67},{67,3},{4,68},{68... | collective-permute-start | bytes 1572872 | tf_op jit(solution)/shard_map/ppermute | solution.py:75
